TPU v7x, 32 devices: a whole 2x2x4 slice. The times are simulated.
32 devices in a mesh: wide: 8 (over z, x), narrow: 4 (over y, core).
Axes of the slice: x: 2, y: 2, z: 4, core: 2. Of those that a mesh axis runs over, the one named last changes fastest.
Arguments:
- atmos_state: bfloat16 [96, 256, 512], P('narrow', 'wide'), may hold values from -6 to 6
- ocean_state: bfloat16 [96, 256, 512], P('narrow', 'wide'), may hold values from -6 to 6
- wet_mask: int32 [96, 256], P('narrow', 'wide'), may hold values 0 or 1
- atmos_kernel: float32 [7, 7, 512], replicated, may hold values from -0.875 to 0.875
- atmos_gain: float32 [512], replicated, may hold values from 0.1 to 1.9
- atmos_inner: bfloat16 [512, 2048], replicated, may hold values from -0.25 to 0.25
- atmos_outer: bfloat16 [2048, 512], replicated, may hold values from -0.125 to 0.125
- ocean_kernel: float32 [7, 7, 512], replicated, may hold values from -0.875 to 0.875
- ocean_gain: float32 [512], replicated, may hold values from 0.1 to 1.9
- ocean_inner: bfloat16 [512, 2048], replicated, may hold values from -0.25 to 0.25
- ocean_outer: bfloat16 [2048, 512], replicated, may hold values from -0.125 to 0.125
- flux_head: bfloat16 [512, 8], replicated, may hold values from -0.25 to 0.25
- flux_lift: bfloat16 [8, 512], replicated, may hold values from -2 to 2
- surface_head: bfloat16 [512, 8], replicated, may hold values from -0.25 to 0.25
- surface_lift: bfloat16 [8, 512], replicated, may hold values from -2 to 2
- flux_source: int32 [4, 8, 48], P('narrow', 'wide'), may hold values from 0 to 71
- flux_target: int32 [4, 8, 48], P('narrow', 'wide'), may hold values from 0 to 5
- flux_weight: float32 [4, 8, 48], P('narrow', 'wide'), may hold values from 0.2 to 1
- surface_source: int32 [4, 8, 48], P('narrow', 'wide'), may hold values from 0 to 71
- surface_target: int32 [4, 8, 48], P('narrow', 'wide'), may hold values from 0 to 5
- surface_weight: float32 [4, 8, 48], P('narrow', 'wide'), may hold values from 0.2 to 1
- atmos_cotangent: bfloat16 [96, 256, 512], P('narrow', 'wide'), may hold values from -6 to 6
- ocean_cotangent: bfloat16 [96, 256, 512], P('narrow', 'wide'), may hold values from -6 to 6
Outputs:
- atmos_next: bfloat16 [96, 256, 512], P('narrow', 'wide')
- ocean_next: bfloat16 [96, 256, 512], P('narrow', 'wide')
- atmos_state_grad: bfloat16 [96, 256, 512], P('narrow', 'wide')
- ocean_state_grad: bfloat16 [96, 256, 512], P('narrow', 'wide')
- atmos_inner_grad: float32 [512, 2048], P(('wide', 'narrow'))
- atmos_outer_grad: float32 [2048, 512], P(('wide', 'narrow'))
- atmos_kernel_grad: float32 [7, 7, 512], replicated
- ocean_inner_grad: float32 [512, 2048], P(('wide', 'narrow'))
- ocean_outer_grad: float32 [2048, 512], P(('wide', 'narrow'))
- ocean_kernel_grad: float32 [7, 7, 512], replicated
Inputs may be any that keep to these rules, and one draw needn't show every extreme that they name: `flux_source`: A value (o * 4 + m) * 6 + s names block s of the tile in latitude row m and longitude column w + o - 1, taken periodically, for a target tile in longitude column w. `flux_target`: block of the target tile that receives the entry. `surface_source`: A value (o * 4 + m) * 6 + s names block s of the tile in latitude row m and longitude column w + o - 1, taken periodically, for a target tile in longitude column w. `surface_target`: block of the target tile that receives the entry. `wet_mask`: 1 marks a sea cell, 0 a land cell.
All inputs are finite; a program needn't handle non-finite values. No bound on the sum of `wet_mask` on one device may be relied on, other than what follows from the above.
Results may differ from a plain program's by a relative error of at most 0.015.
Values may be sent and summed in bfloat16 or wider, within the bound.
No kernel may reach another device: no remote copies, remote signals or barrier semaphores. Data moves between devices by JAX's collectives and lax.ppermute only.
A program may use at most 192 MiB of HBM per device.

v0:
```python
import jax
import jax.numpy as jnp
from jax import lax
from jax.sharding import PartitionSpec as P

KERNEL = 7


norm_eps = 1e-06
grad_scale = 256.0
highest = lax.Precision.HIGHEST


def from_partner(shard, axis, distance):
    return lax.ppermute(shard, axis, [(i, i ^ 1 << distance) for i in range(lax.axis_size(axis))])


def extended(cells, sides, width, closed):
    for axis, dim in sides:
        count = lax.axis_size(axis)
        ends = count if closed else count - 1
        head = lax.slice_in_dim(cells, 0, width, axis=dim)
        tail = lax.slice_in_dim(cells, cells.shape[dim] - width, cells.shape[dim], axis=dim)
        cells = jnp.concatenate(
            [
                lax.ppermute(tail, axis, [(i, (i + 1) % count) for i in range(ends)]),
                cells,
                lax.ppermute(head, axis, [((i + 1) % count, i) for i in range(ends)]),
            ],
            axis=dim,
        )
    return cells


def normal_cdf(values):
    return 0.5 * (1.0 + lax.erf(values * 0.7071067811865476))


def normal_density(values):
    return jnp.exp(-0.5 * values * values) * 0.3989422804014327


def at_fold():
    return lax.axis_index("narrow") == lax.axis_size("narrow") - 1


def fold_rows(top_band):
    levels = lax.axis_size("wide").bit_length() - 1
    for bit_place in range(levels):
        top_band = from_partner(top_band, "wide", bit_place)
    return top_band[::-1, ::-1]


def extend(fields, folded):
    margin = KERNEL // 2
    row_count = fields.shape[0]
    beside = extended(fields, (("wide", 1),), margin, True)
    padded = extended(beside, (("narrow", 0),), margin, False)
    if folded:
        mirror = fold_rows(padded[row_count : row_count + margin])
        upper_rows = jnp.where(at_fold(), mirror, padded[row_count + margin :])
        padded = jnp.concatenate([padded[: row_count + margin], upper_rows], axis=0)
    return padded


def apply_kernel(padded, kernel, row_count, col_count, flipped):
    last_tap = KERNEL - 1
    running = jnp.zeros((row_count, col_count, kernel.shape[-1]), jnp.float32)
    for row_tap in range(KERNEL):
        for col_tap in range(KERNEL):
            row_from = last_tap - row_tap if flipped else row_tap
            col_from = last_tap - col_tap if flipped else col_tap
            window = padded[row_from : row_from + row_count, col_from : col_from + col_count]
            running = running + window * kernel[row_tap, col_tap]
    return running


def block_forward(start_field, kernel, norm_gain, inner_weight, outer_weight, folded):
    row_count, col_count, channels = start_field.shape
    padded = extend(start_field, folded)
    mixed_taps = apply_kernel(padded, kernel, row_count, col_count, False)
    center = mixed_taps - jnp.mean(mixed_taps, axis=-1, keepdims=True)
    inverse = lax.rsqrt(jnp.mean(center * center, axis=-1, keepdims=True) + norm_eps)
    scaled = center * inverse
    normed = (scaled * norm_gain).astype(jnp.bfloat16).reshape(-1, channels)
    before = jnp.dot(normed, inner_weight, preferred_element_type=jnp.float32)
    hidden = (before * normal_cdf(before)).astype(jnp.bfloat16)
    branch = jnp.dot(hidden, outer_weight, preferred_element_type=jnp.float32).reshape(
        row_count, col_count, channels
    )
    return (branch, (padded, scaled, inverse, normed, before, hidden))


def block_backward(stored, kernel, norm_gain, inner_weight, outer_weight, incoming, folded):
    padded, scaled, inverse, normed, before, hidden = stored
    row_count, col_count, channels = scaled.shape
    margin = KERNEL // 2
    rounded = incoming.astype(jnp.bfloat16)
    flat_round = rounded.reshape(-1, channels)
    d_hidden = jnp.einsum("cd,fd->cf", flat_round, outer_weight, preferred_element_type=jnp.float32)
    slopes = normal_cdf(before) + before * normal_density(before)
    d_before = (d_hidden * slopes).astype(jnp.bfloat16)
    d_normed = jnp.einsum("cf,df->cd", d_before, inner_weight, preferred_element_type=jnp.float32)
    d_scaled = d_normed.reshape(row_count, col_count, channels) * norm_gain
    mean_grad = jnp.mean(d_scaled, axis=-1, keepdims=True)
    mean_cross = jnp.mean(d_scaled * scaled, axis=-1, keepdims=True)
    d_taps = (inverse * (d_scaled - mean_grad - scaled * mean_cross)).astype(jnp.bfloat16)
    kernel_rows = []
    for row_tap in range(KERNEL):
        for col_tap in range(KERNEL):
            window = padded[row_tap : row_tap + row_count, col_tap : col_tap + col_count]
            kernel_rows.append(
                jnp.einsum("rcd,rcd->d", d_taps, window, preferred_element_type=jnp.float32)
            )
    kernel_term = jnp.stack(kernel_rows).reshape(KERNEL, KERNEL, channels)
    grad_padded = extend(d_taps, folded)
    if folded:
        upper_rows = grad_padded[row_count + margin :]
        blank_rows = jnp.zeros_like(upper_rows)
        top_part = jnp.where(at_fold(), upper_rows, blank_rows)
        lower_rows = jnp.concatenate(
            [grad_padded[: row_count + margin], jnp.where(at_fold(), blank_rows, upper_rows)],
            axis=0,
        )
        spread = apply_kernel(lower_rows, kernel, row_count, col_count, True)
        fold_pad = jnp.concatenate([jnp.zeros_like(grad_padded[: 2 * margin]), top_part], axis=0)
        fold_part = apply_kernel(fold_pad, kernel, margin, col_count, False)
        spread = spread.at[row_count - margin :].add(fold_part)
    else:
        spread = apply_kernel(grad_padded, kernel, row_count, col_count, True)
    return (incoming + spread, (normed, d_before, hidden, flat_round, kernel_term))


def remap_apply(fields, sources, targets, weights):
    lat_count = lax.axis_size("narrow")
    block_count = fields.shape[0]
    column = lax.all_gather(fields[None], "narrow", axis=0, tiled=True)
    beside_all = extended(column, (("wide", 0),), lat_count, True)
    flat_blocks = beside_all.reshape(-1, fields.shape[1], fields.shape[2])
    picked = flat_blocks[sources].astype(jnp.float32)
    placing = (targets[:, None] == jnp.arange(block_count, dtype=jnp.int32)[None, :]).astype(
        jnp.float32
    ) * weights[:, None]
    return jnp.einsum("eb,ekp->bkp", placing, picked, precision=highest)


def remap_adjoint(gradient, sources, targets, weights):
    lat_count = lax.axis_size("narrow")
    block_count = gradient.shape[0]
    placing = (targets[:, None] == jnp.arange(block_count, dtype=jnp.int32)[None, :]).astype(
        jnp.float32
    ) * weights[:, None]
    d_picked = jnp.einsum("eb,bkp->ekp", placing, gradient, precision=highest)
    choose = (
        sources[:, None] == jnp.arange(3 * lat_count * block_count, dtype=jnp.int32)[None, :]
    ).astype(jnp.float32)
    d_flat = jnp.einsum("ef,ekp->fkp", choose, d_picked, precision=highest)
    d_flat = d_flat.reshape(3 * lat_count, block_count, gradient.shape[1], gradient.shape[2])
    outward = jnp.concatenate([d_flat[:lat_count], d_flat[2 * lat_count :]], axis=0)
    returned = extended(outward.astype(jnp.bfloat16), (("wide", 0),), lat_count, True).astype(
        outward.dtype
    )
    column = d_flat[lat_count : 2 * lat_count] + returned[:lat_count] + returned[3 * lat_count :]
    own_part = lax.psum_scatter(
        column.astype(jnp.bfloat16), "narrow", scatter_dimension=0, tiled=True
    ).astype(jnp.float32)
    return own_part[0]


def to_cells(blocks, lift_weight, row_count, col_count):
    lifted = jnp.einsum("bkp,kd->bpd", blocks, lift_weight.astype(jnp.float32), precision=highest)
    return lifted.reshape(row_count, col_count, lift_weight.shape[1])


def lift_back(gradient, lift_weight):
    return jnp.einsum(
        "bpd,kd->bkp",
        gradient.reshape(-1, 128, lift_weight.shape[1]),
        lift_weight.astype(jnp.float32),
        precision=highest,
    )


def head_back(gradient, head_weight, row_count, col_count):
    spread = jnp.einsum("bkp,dk->bpd", gradient, head_weight.astype(jnp.float32), precision=highest)
    return spread.reshape(row_count, col_count, head_weight.shape[0])


def weight_sums(records):
    channels = records[0][0].shape[1]
    hidden_units = records[0][2].shape[1]
    stacked = jnp.stack([record[4] for record in records])
    pieces = [
        lax.dot_general(
            record[0], record[1], (((0,), (0,)), ((), ())), preferred_element_type=jnp.float32
        )
        for record in records
    ]
    inner_sums = lax.psum_scatter(
        jnp.concatenate(pieces, axis=1), ("wide", "narrow"), scatter_dimension=0, tiled=True
    )
    pieces = [
        lax.dot_general(
            record[2], record[3], (((0,), (0,)), ((), ())), preferred_element_type=jnp.float32
        )
        for record in records
    ]
    outer_sums = lax.psum_scatter(
        jnp.concatenate(pieces, axis=1), ("wide", "narrow"), scatter_dimension=0, tiled=True
    )
    kernel_sums = lax.psum(stacked, ("wide", "narrow"))
    results = []
    for grid_index in range(len(records)):
        inner_part = (
            inner_sums[:, grid_index * hidden_units : (grid_index + 1) * hidden_units] / grad_scale
        )
        outer_part = outer_sums[:, grid_index * channels : (grid_index + 1) * channels] / grad_scale
        results.append((inner_part, outer_part, kernel_sums[grid_index] / grad_scale))
    return results


def per_device(
    atmos_state,
    ocean_state,
    wet_mask,
    atmos_kernel,
    atmos_gain,
    atmos_inner,
    atmos_outer,
    ocean_kernel,
    ocean_gain,
    ocean_inner,
    ocean_outer,
    flux_head,
    flux_lift,
    surface_head,
    surface_lift,
    flux_source,
    flux_target,
    flux_weight,
    surface_source,
    surface_target,
    surface_weight,
    atmos_cotangent,
    ocean_cotangent,
):
    row_count, col_count, channels = atmos_state.shape
    wet_cells = wet_mask.astype(jnp.float32)[:, :, None]
    flux_lists = (flux_source.reshape(-1), flux_target.reshape(-1), flux_weight.reshape(-1))
    surface_lists = (
        surface_source.reshape(-1),
        surface_target.reshape(-1),
        surface_weight.reshape(-1),
    )
    surface = jnp.einsum(
        "bpd,dk->bkp",
        ocean_state.reshape(-1, 128, channels),
        surface_head,
        preferred_element_type=jnp.float32,
    ).astype(jnp.bfloat16)
    to_atmos = remap_apply(surface, surface_lists[0], surface_lists[1], surface_lists[2])
    atmos_start = (atmos_state + to_cells(to_atmos, surface_lift, row_count, col_count)).astype(
        jnp.bfloat16
    )
    atmos_branch, atmos_stored = block_forward(
        atmos_start, atmos_kernel, atmos_gain, atmos_inner, atmos_outer, False
    )
    atmos_next = (atmos_start + atmos_branch).astype(jnp.bfloat16)
    fluxes = jnp.einsum(
        "bpd,dk->bkp",
        atmos_next.reshape(-1, 128, channels),
        flux_head,
        preferred_element_type=jnp.float32,
    ).astype(jnp.bfloat16)
    to_ocean = remap_apply(fluxes, flux_lists[0], flux_lists[1], flux_lists[2])
    ocean_start = (
        (ocean_state + to_cells(to_ocean, flux_lift, row_count, col_count)) * wet_cells
    ).astype(jnp.bfloat16)
    ocean_branch, ocean_stored = block_forward(
        ocean_start, ocean_kernel, ocean_gain, ocean_inner, ocean_outer, True
    )
    ocean_next = ((ocean_start + ocean_branch) * wet_cells).astype(jnp.bfloat16)
    ocean_total = ocean_cotangent * wet_cells
    ocean_start_grad, ocean_record = block_backward(
        ocean_stored, ocean_kernel, ocean_gain, ocean_inner, ocean_outer, ocean_total, True
    )
    ocean_start_grad = ocean_start_grad * wet_cells
    flux_grad = remap_adjoint(
        lift_back(ocean_start_grad, flux_lift), flux_lists[0], flux_lists[1], flux_lists[2]
    )
    atmos_total = atmos_cotangent + head_back(flux_grad, flux_head, row_count, col_count)
    atmos_start_grad, atmos_record = block_backward(
        atmos_stored, atmos_kernel, atmos_gain, atmos_inner, atmos_outer, atmos_total, False
    )
    atmos_state_grad = atmos_start_grad.astype(jnp.bfloat16)
    surface_grad = remap_adjoint(
        lift_back(atmos_start_grad, surface_lift),
        surface_lists[0],
        surface_lists[1],
        surface_lists[2],
    )
    ocean_state_grad = (
        ocean_start_grad + head_back(surface_grad, surface_head, row_count, col_count)
    ).astype(jnp.bfloat16)
    atmos_sums, ocean_sums = weight_sums([atmos_record, ocean_record])
    return (
        atmos_next,
        ocean_next,
        atmos_state_grad,
        ocean_state_grad,
        atmos_sums[0],
        atmos_sums[1],
        atmos_sums[2],
        ocean_sums[0],
        ocean_sums[1],
        ocean_sums[2],
    )


def solution(mesh):
    return jax.shard_map(
        per_device,
        mesh=mesh,
        in_specs=(
            P("narrow", "wide", None),
            P("narrow", "wide", None),
            P("narrow", "wide"),
            P(),
            P(),
            P(),
            P(),
            P(),
            P(),
            P(),
            P(),
            P(),
            P(),
            P(),
            P(),
            P("narrow", "wide", None),
            P("narrow", "wide", None),
            P("narrow", "wide", None),
            P("narrow", "wide", None),
            P("narrow", "wide", None),
            P("narrow", "wide", None),
            P("narrow", "wide", None),
            P("narrow", "wide", None),
        ),
        out_specs=(
            P("narrow", "wide", None),
            P("narrow", "wide", None),
            P("narrow", "wide", None),
            P("narrow", "wide", None),
            P(("wide", "narrow"), None),
            P(("wide", "narrow"), None),
            P(),
            P(("wide", "narrow"), None),
            P(("wide", "narrow"), None),
            P(),
        ),
        check_vma=False,
    )
```

profile of v0, /device:TPU:0, one launch (start us, length us, event | category | flops | bytes accessed | tf_op | source)
XLA Modules:
  0.0 770.6 jit_solution(12066809997903587967)
XLA Ops:
  8.9 6.2 all-gather
  15.1 5.0 collective-permute-start.1
  21.4 1.8 fusion.265
  24.0 2.8 collective-permute-done
  29.7 4.7 collective-permute-start.3
  39.7 3.6 collective-permute-done.5
  44.3 12.8 %fusion.252 = (f32[24,32]{1,0:T(8,128)S(1)}, f32[24,32,512]{2,1,0:T(8,128)S(1)}) fusion(f32[512]{0:T(512)} %bitcast.256, bf16[27,38,512]{2,1,0:T(8,128)(2,1)S(1)} %get-tuple-element.201, f32[512]{0:T(512)} %bitcast.255, f32[512]{0:T(512)S(1)} %bitcast.916, f32[512]{0:T(512)S(1)} %bitcast.918, f32[512]{0:T(512)S(1)} %bitcast.920, f32[512]{0:T(512)S(1)} %bitcast.922, ...), kind=kLoop, calls=%fused_computation.498 | loop fusion | flops 64879872 | bytes 35640320 | tf_op jit(solution)/shard_map/reduce_sum | solution.py:82
  59.3 4.3 multiply_convert_fusion.1
  63.6 1.8 fusion.270
  66.9 7.4 all-gather.1
  74.3 4.7 collective-permute-start.7
  80.8 5.0 collective-permute-done.6
  90.8 1.8 fusion.256
  92.6 4.7 collective-permute-start.9
  97.3 2.8 collective-permute-done.8
  101.8 1.8 fusion.261
  103.6 3.3 collective-permute-done.11
  109.9 1.9 collective-permute-done.12
  111.8 2.1 collective-permute-start.13
  115.5 3.8 collective-permute-start.10
  119.3 2.0 collective-permute-done.13
  121.3 2.8 rev.6
  125.4 2.8 maximum_maximum_fusion.1
  128.6 14.8 %fusion.250 = (f32[24,32]{1,0:T(8,128)S(1)}, f32[24,32,512]{2,1,0:T(8,128)S(1)}) fusion(f32[512]{0:T(512)S(1)} %bitcast.824, bf16[27,38,512]{2,1,0:T(8,128)(2,1)S(1)} %get-tuple-element.197, f32[512]{0:T(512)S(1)} %bitcast.827, f32[512]{0:T(512)S(1)} %bitcast.767, f32[512]{0:T(512)S(1)} %bitcast.770, f32[512]{0:T(512)S(1)} %bitcast.773, ...), kind=kLoop, calls=%fused_computation.497 | loop fusion | flops 64879872 | bytes 35640320 | tf_op jit(solution)/shard_map/reduce_sum | solution.py:82
  144.5 3.9 multiply_convert_fusion
  148.4 3.9 fusion.5
  152.3 3.0 multiply_reduce_fusion.3
  155.4 2.5 multiply_reduce_fusion.2
  158.4 6.4 fusion.162
  164.9 3.6 collective-permute-start.16
  170.7 5.3 collective-permute-done.15
  176.8 4.6 fusion.134
  181.9 6.9 fusion.144
  190.7 3.0 fusion.271
  193.6 3.4 collective-permute-start.21
  197.1 2.7 collective-permute-done.19
  204.4 13.0 %multiply_add_fusion = f32[24,32,512]{2,1,0:T(8,128)S(1)} fusion(bf16[24,32,512]{2,1,0:T(8,128)(2,1)S(1)} %get-tuple-element.181, bf16[24,3,512]{2,1,0:T(4,128)(2,1)S(1)} %copy-done.33, bf16[24,3,512]{2,1,0:T(4,128)(2,1)S(1)} %copy-done.31, bf16[27,38,512]{2,1,0:T(8,128)(2,1)S(1)} %get-tuple-element.193, bf16[27,38,512]{2,1,0:T(8,128)(2,1)S(1)} %get-tuple-element.192, ...), kind=kLoop, calls=%fused_computation.281 | loop fusion | flops 64487424 | bytes 35637248 | tf_op jit(solution)/shard_map/add | solution.py:74
  218.6 2.6 add_multiply_fusion.2
  222.9 2.3 collective-permute-start.23
  225.2 3.9 fusion.275
  229.2 3.2 collective-permute-done.22
  236.4 16.1 %reduce-scatter.7.cloned.1.call-done = bf16[1,6,8,128]{3,2,1,0:T(8,128)(2,1)} async-done(((bf16[4,6,8,128]{3,2,1,0:T(8,128)(2,1)}), bf16[1,6,8,128]{3,2,1,0:T(8,128)(2,1)}) %reduce-scatter.7.cloned.1.call-update) | async-done | bytes 12304 | tf_op jit(solution)/shard_map/reduce_scatter | solution.py:164
  253.3 2.9 fusion.268
  256.2 6.2 fusion.11
  262.5 3.0 multiply_reduce_fusion.1
  265.6 2.0 multiply_reduce_fusion
  267.8 5.8 fusion.113
  273.5 3.9 fusion.85
  279.1 3.2 collective-permute-start.25
  282.3 3.2 fusion.95
  285.5 3.9 fusion.274
  290.8 3.4 collective-permute-start.27
  297.0 14.0 %fusion.249 = (bf16[24,32,512]{2,1,0:T(8,128)(2,1)}, f32[24,32,512]{2,1,0:T(8,128)S(1)}) fusion(f32[24,32,512]{2,1,0:T(8,128)S(1)} %copy-done.21, f32[512]{0:T(512)} %bitcast.256, bf16[27,38,512]{2,1,0:T(8,128)(2,1)S(1)} %get-tuple-element.189, f32[512]{0:T(512)} %bitcast.255, f32[512]{0:T(512)S(1)} %bitcast.917, f32[512]{0:T(512)S(1)} %bitcast.919, ...), kind=kLoop, calls=%fused_computation.496 | loop fusion | flops 65273856 | bytes 37996544 | tf_op jit(solution)/shard_map/convert_element_type | solution.py:295
  316.8 4.2 collective-permute-done.28
  321.7 7.9 %pad_maximum_fusion.1 = f32[2048,1024]{0,1:T(8,128)} fusion(f32[2048,512]{0,1:T(8,128)} %fusion.275, f32[2048,512]{0,1:T(8,128)} %fusion.274), kind=kLoop, calls=%fused_computation.103 | loop fusion | flops 2097152 | bytes 16777216 | tf_op jit(solution)/shard_map/concatenate | solution.py:209
  329.6 9.3 %copy.767 = f32[2048,1024]{1,0:T(8,128)} copy(f32[2048,1024]{0,1:T(8,128)} %pad_maximum_fusion.1) | data formatting | bytes 16777216
  339.0 1.8 copy-done.18
  340.9 3.1 fusion.273
  344.0 1.9 fusion.272
  345.9 3.8 pad_maximum_fusion
  349.7 90.8 %all-reduce.3.cloned.1.call-done = f32[2,7,7,512]{3,2,1,0:T(8,128)} async-done(((f32[2,7,7,512]{3,2,1,0:T(8,128)}), f32[2,7,7,512]{3,2,1,0:T(8,128)}) %all-reduce.3.cloned.1.call-update) | async-done | bytes 200720 | tf_op jit(solution)/shard_map/psum | solution.py:211
  442.2 21.7 %reduce-scatter.9.cloned.1.call-done = bf16[1,6,8,128]{3,2,1,0:T(8,128)(2,1)} async-done(((bf16[4,6,8,128]{3,2,1,0:T(8,128)(2,1)}), bf16[1,6,8,128]{3,2,1,0:T(8,128)(2,1)}) %reduce-scatter.9.cloned.1.call-update) | async-done | bytes 12304 | tf_op jit(solution)/shard_map/reduce_scatter | solution.py:164
  466.0 149.0 %reduce-scatter.13.cloned.1.call-done = f32[64,1024]{1,0:T(8,128)} async-done(((f32[2048,1024]{1,0:T(8,128)}), f32[64,1024]{1,0:T(8,128)}) %reduce-scatter.13.cloned.1.call-update) | async-done | bytes 262160
  617.9 144.1 %reduce-scatter.11.cloned.1.call-done = f32[16,4096]{1,0:T(8,128)} async-done(((f32[512,4096]{1,0:T(8,128)}), f32[16,4096]{1,0:T(8,128)}) %reduce-scatter.11.cloned.1.call-update) | async-done | bytes 262160 | tf_op jit(solution)/shard_map/reduce_scatter | solution.py:199
  (729 shorter events, 67.6 us)
Async XLA Ops:
  7.2 137.3 %copy-start = (bf16[512,2048]{1,0:T(8,128)(2,1)S(1)}, bf16[512,2048]{1,0:T(8,128)(2,1)}, u32[]{:S(2)}) copy-start(bf16[512,2048]{1,0:T(8,128)(2,1)} %param.34) | copy-start | bytes 6291460
  7.2 245.3 %reduce-scatter.7.cloned.1.call-start = ((), (), s32[]{:S(2)}) async-start(), calls=%async_computation.4 | async-start | bytes 61440 | tf_op jit(solution)/shard_map/reduce_scatter | solution.py:164
  7.2 21.9 %copy-start.34 = (bf16[24,32,512]{2,1,0:T(8,128)(2,1)S(1)}, bf16[24,32,512]{2,1,0:T(8,128)(2,1)}, u32[]{:S(2)}) copy-start(bf16[24,32,512]{2,1,0:T(8,128)(2,1)} %param.25) | copy-start | bytes 2359300
  15.1 9.0 %collective-permute-start.1 = (bf16[4,6,8,128]{3,2,1,0:T(8,128)(2,1)S(1)}, bf16[4,6,8,128]{3,2,1,0:T(8,128)(2,1)S(1)}, u32[]{:S(2)}, u32[]{:S(2)}) collective-permute-start(bf16[4,6,8,128]{3,2,1,0:T(8,128)(2,1)S(1)} %bitcast.753), channel_id=1, source_target_pairs={{4,0},{8,4},{12,8},{16,12},{20,16},{24,20},{28,24},{0,28},{5,1},{9... | collective-permute-start | bytes 147464 | tf_op jit(solution)/shard_map/ppermute | solution.py:28
  20.1 6.8 collective-permute-start
  21.2 22.7 %copy-start.157 = (f32[1,1,512]{2,1,0:T(1,128)}, f32[1,1,512]{2,1,0:T(1,128)S(1)}, u32[]{:S(2)}) copy-start(f32[1,1,512]{2,1,0:T(1,128)S(1)} %get-tuple-element.273) | copy-start | bytes 6148
  21.3 22.7 %copy-start.159 = (f32[1,1,512]{2,1,0:T(1,128)}, f32[1,1,512]{2,1,0:T(1,128)S(1)}, u32[]{:S(2)}) copy-start(f32[1,1,512]{2,1,0:T(1,128)S(1)} %get-tuple-element.274) | copy-start | bytes 6148
  21.3 22.7 %copy-start.161 = (f32[1,1,512]{2,1,0:T(1,128)}, f32[1,1,512]{2,1,0:T(1,128)S(1)}, u32[]{:S(2)}) copy-start(f32[1,1,512]{2,1,0:T(1,128)S(1)} %get-tuple-element.275) | copy-start | bytes 6148
  21.3 22.7 %copy-start.163 = (f32[1,1,512]{2,1,0:T(1,128)}, f32[1,1,512]{2,1,0:T(1,128)S(1)}, u32[]{:S(2)}) copy-start(f32[1,1,512]{2,1,0:T(1,128)S(1)} %get-tuple-element.276) | copy-start | bytes 6148
  21.3 22.7 %copy-start.165 = (f32[1,1,512]{2,1,0:T(1,128)}, f32[1,1,512]{2,1,0:T(1,128)S(1)}, u32[]{:S(2)}) copy-start(f32[1,1,512]{2,1,0:T(1,128)S(1)} %get-tuple-element.277) | copy-start | bytes 6148
  21.3 22.7 %copy-start.167 = (f32[1,1,512]{2,1,0:T(1,128)}, f32[1,1,512]{2,1,0:T(1,128)S(1)}, u32[]{:S(2)}) copy-start(f32[1,1,512]{2,1,0:T(1,128)S(1)} %get-tuple-element.278) | copy-start | bytes 6148
  21.3 22.7 %copy-start.169 = (f32[1,1,512]{2,1,0:T(1,128)}, f32[1,1,512]{2,1,0:T(1,128)S(1)}, u32[]{:S(2)}) copy-start(f32[1,1,512]{2,1,0:T(1,128)S(1)} %get-tuple-element.279) | copy-start | bytes 6148
  21.3 22.7 %copy-start.171 = (f32[1,1,512]{2,1,0:T(1,128)}, f32[1,1,512]{2,1,0:T(1,128)S(1)}, u32[]{:S(2)}) copy-start(f32[1,1,512]{2,1,0:T(1,128)S(1)} %get-tuple-element.280) | copy-start | bytes 6148
  21.3 22.7 %copy-start.173 = (f32[1,1,512]{2,1,0:T(1,128)}, f32[1,1,512]{2,1,0:T(1,128)S(1)}, u32[]{:S(2)}) copy-start(f32[1,1,512]{2,1,0:T(1,128)S(1)} %get-tuple-element.281) | copy-start | bytes 6148
  21.3 22.7 %copy-start.175 = (f32[1,1,512]{2,1,0:T(1,128)}, f32[1,1,512]{2,1,0:T(1,128)S(1)}, u32[]{:S(2)}) copy-start(f32[1,1,512]{2,1,0:T(1,128)S(1)} %get-tuple-element.282) | copy-start | bytes 6148
  21.3 22.7 %copy-start.177 = (f32[1,1,512]{2,1,0:T(1,128)}, f32[1,1,512]{2,1,0:T(1,128)S(1)}, u32[]{:S(2)}) copy-start(f32[1,1,512]{2,1,0:T(1,128)S(1)} %get-tuple-element.283) | copy-start | bytes 6148
  21.4 22.7 %copy-start.179 = (f32[1,1,512]{2,1,0:T(1,128)}, f32[1,1,512]{2,1,0:T(1,128)S(1)}, u32[]{:S(2)}) copy-start(f32[1,1,512]{2,1,0:T(1,128)S(1)} %get-tuple-element.284) | copy-start | bytes 6148
  21.4 22.7 %copy-start.181 = (f32[1,1,512]{2,1,0:T(1,128)}, f32[1,1,512]{2,1,0:T(1,128)S(1)}, u32[]{:S(2)}) copy-start(f32[1,1,512]{2,1,0:T(1,128)S(1)} %get-tuple-element.285) | copy-start | bytes 6148
  21.4 22.7 %copy-start.183 = (f32[1,1,512]{2,1,0:T(1,128)}, f32[1,1,512]{2,1,0:T(1,128)S(1)}, u32[]{:S(2)}) copy-start(f32[1,1,512]{2,1,0:T(1,128)S(1)} %get-tuple-element.286) | copy-start | bytes 6148
  21.4 22.7 %copy-start.185 = (f32[1,1,512]{2,1,0:T(1,128)}, f32[1,1,512]{2,1,0:T(1,128)S(1)}, u32[]{:S(2)}) copy-start(f32[1,1,512]{2,1,0:T(1,128)S(1)} %get-tuple-element.287) | copy-start | bytes 6148
  21.4 22.7 %copy-start.187 = (f32[1,1,512]{2,1,0:T(1,128)}, f32[1,1,512]{2,1,0:T(1,128)S(1)}, u32[]{:S(2)}) copy-start(f32[1,1,512]{2,1,0:T(1,128)S(1)} %get-tuple-element.288) | copy-start | bytes 6148
  21.4 22.7 %copy-start.189 = (f32[1,1,512]{2,1,0:T(1,128)}, f32[1,1,512]{2,1,0:T(1,128)S(1)}, u32[]{:S(2)}) copy-start(f32[1,1,512]{2,1,0:T(1,128)S(1)} %get-tuple-element.289) | copy-start | bytes 6148
  21.4 22.7 %copy-start.191 = (f32[1,1,512]{2,1,0:T(1,128)}, f32[1,1,512]{2,1,0:T(1,128)S(1)}, u32[]{:S(2)}) copy-start(f32[1,1,512]{2,1,0:T(1,128)S(1)} %get-tuple-element.290) | copy-start | bytes 6148
  21.4 22.7 %copy-start.193 = (f32[1,1,512]{2,1,0:T(1,128)}, f32[1,1,512]{2,1,0:T(1,128)S(1)}, u32[]{:S(2)}) copy-start(f32[1,1,512]{2,1,0:T(1,128)S(1)} %get-tuple-element.291) | copy-start | bytes 6148
  29.5 35.9 %copy-start.13 = (bf16[24,32,512]{2,1,0:T(8,128)(2,1)}, bf16[24,32,512]{2,1,0:T(8,128)(2,1)S(1)}, u32[]{:S(2)}) copy-start(bf16[24,32,512]{2,1,0:T(8,128)(2,1)S(1)} %add_convert_fusion.1) | copy-start | bytes 2359300
  29.6 7.4 collective-permute-start.2
  29.7 7.3 collective-permute-start.3
  37.1 2.6 collective-permute-start.4
  38.4 5.0 collective-permute-start.5
  65.4 23.0 %copy-start.44 = (bf16[8,512]{1,0:T(8,128)(2,1)S(1)}, bf16[8,512]{1,0:T(8,128)(2,1)}, u32[]{:S(2)}) copy-start(bf16[8,512]{1,0:T(8,128)(2,1)} %param.37) | copy-start | bytes 24580
  74.3 6.5 collective-permute-start.7
  79.0 6.8 collective-permute-start.6
  92.6 7.5 collective-permute-start.8
  92.6 7.5 collective-permute-start.9
  101.8 5.1 collective-permute-start.11
  103.6 24.6 %copy-start.50 = (f32[1,1,512]{2,1,0:T(1,128)}, f32[1,1,512]{2,1,0:T(1,128)S(1)}, u32[]{:S(2)}) copy-start(f32[1,1,512]{2,1,0:T(1,128)S(1)} %get-tuple-element.228) | copy-start | bytes 6148
  103.6 24.6 %copy-start.52 = (f32[1,1,512]{2,1,0:T(1,128)}, f32[1,1,512]{2,1,0:T(1,128)S(1)}, u32[]{:S(2)}) copy-start(f32[1,1,512]{2,1,0:T(1,128)S(1)} %get-tuple-element.229) | copy-start | bytes 6148
  103.6 24.6 %copy-start.54 = (f32[1,1,512]{2,1,0:T(1,128)}, f32[1,1,512]{2,1,0:T(1,128)S(1)}, u32[]{:S(2)}) copy-start(f32[1,1,512]{2,1,0:T(1,128)S(1)} %get-tuple-element.230) | copy-start | bytes 6148
  106.9 4.9 collective-permute-start.12
  108.6 15.4 %collective-permute-start.14 = (bf16[3,38,512]{2,1,0:T(8,128)(2,1)}, bf16[3,38,512]{2,1,0:T(8,128)(2,1)}, u32[]{:S(2)}, u32[]{:S(2)}) collective-permute-start(bf16[3,38,512]{2,1,0:T(8,128)(2,1)} %get-tuple-element.198), channel_id=1, source_target_pairs={{1,0},{2,1},{3,2},{5,4},{6,5},{7,6},{9,8},{10,9},{11,10},{13,12},{... | collective-permute-start | bytes 350216 | tf_op jit(solution)/shard_map/ppermute | solution.py:28
  111.8 9.5 %collective-permute-start.13 = (bf16[3,38,512]{2,1,0:T(8,128)(2,1)S(1)}, bf16[3,38,512]{2,1,0:T(8,128)(2,1)}, u32[]{:S(2)}, u32[]{:S(2)}) collective-permute-start(bf16[3,38,512]{2,1,0:T(8,128)(2,1)S(1)} %collective-permute-done.12), channel_id=1, source_target_pairs={{0,16},{4,20},{8,24},{12,28},{16,0},{20,4},{24,8},{28,12},{1,17},{... | collective-permute-start | bytes 350216 | tf_op jit(solution)/shard_map/ppermute | solution.py:15
  115.5 9.9 %collective-permute-start.10 = (bf16[3,38,512]{2,1,0:T(8,128)(2,1)}, bf16[3,38,512]{2,1,0:T(8,128)(2,1)}, u32[]{:S(2)}, u32[]{:S(2)}) collective-permute-start(bf16[3,38,512]{2,1,0:T(8,128)(2,1)} %get-tuple-element.199), channel_id=1, source_target_pairs={{0,1},{1,2},{2,3},{4,5},{5,6},{6,7},{8,9},{9,10},{10,11},{12,13},{... | collective-permute-start | bytes 350216 | tf_op jit(solution)/shard_map/ppermute | solution.py:26
  164.9 5.8 collective-permute-start.16
  168.5 7.5 collective-permute-start.15
  176.8 5.1 collective-permute-start.17
  181.9 8.2 %collective-permute-start.18 = (bf16[3,38,512]{2,1,0:T(8,128)(2,1)S(1)}, bf16[3,38,512]{2,1,0:T(8,128)(2,1)S(1)}, u32[]{:S(2)}, u32[]{:S(2)}) collective-permute-start(bf16[3,38,512]{2,1,0:T(8,128)(2,1)S(1)} %collective-permute-done.17), channel_id=1, source_target_pairs={{0,8},{4,12},{8,0},{12,4},{16,24},{20,28},{24,16},{28,20},{1,9},{5... | collective-permute-start | bytes 350216 | tf_op jit(solution)/shard_map/ppermute | solution.py:15
  188.8 12.3 %collective-permute-start.20 = (bf16[3,38,512]{2,1,0:T(8,128)(2,1)}, bf16[3,38,512]{2,1,0:T(8,128)(2,1)}, u32[]{:S(2)}, u32[]{:S(2)}) collective-permute-start(bf16[3,38,512]{2,1,0:T(8,128)(2,1)} %get-tuple-element.194), channel_id=1, source_target_pairs={{1,0},{2,1},{3,2},{5,4},{6,5},{7,6},{9,8},{10,9},{11,10},{13,12},{... | collective-permute-start | bytes 350216 | tf_op jit(solution)/shard_map/ppermute | solution.py:28
  190.1 9.6 %collective-permute-start.19 = (bf16[3,38,512]{2,1,0:T(8,128)(2,1)S(1)}, bf16[3,38,512]{2,1,0:T(8,128)(2,1)S(1)}, u32[]{:S(2)}, u32[]{:S(2)}) collective-permute-start(bf16[3,38,512]{2,1,0:T(8,128)(2,1)S(1)} %collective-permute-done.18), channel_id=1, source_target_pairs={{0,16},{4,20},{8,24},{12,28},{16,0},{20,4},{24,8},{28,12},{1,17},{... | collective-permute-start | bytes 350216 | tf_op jit(solution)/shard_map/ppermute | solution.py:15
  193.6 8.4 %collective-permute-start.21 = (bf16[3,38,512]{2,1,0:T(8,128)(2,1)}, bf16[3,38,512]{2,1,0:T(8,128)(2,1)}, u32[]{:S(2)}, u32[]{:S(2)}) collective-permute-start(bf16[3,38,512]{2,1,0:T(8,128)(2,1)} %get-tuple-element.195), channel_id=1, source_target_pairs={{0,1},{1,2},{2,3},{4,5},{5,6},{6,7},{8,9},{9,10},{10,11},{12,13},{... | collective-permute-start | bytes 350216 | tf_op jit(solution)/shard_map/ppermute | solution.py:26
  222.9 6.2 collective-permute-start.23
  225.2 7.1 collective-permute-start.22
  233.4 207.1 %all-reduce.3.cloned.1.call-start = ((), (), s32[]{:S(2)}) async-start(), calls=%async_computation.7 | async-start | bytes 458752 | tf_op jit(solution)/shard_map/psum | solution.py:211
  277.6 11.8 %collective-permute-start.24 = (bf16[24,3,512]{2,1,0:T(4,128)(2,1)S(1)}, bf16[24,3,512]{2,1,0:T(4,128)(2,1)S(1)}, u32[]{:S(2)}, u32[]{:S(2)}) collective-permute-start(bf16[24,3,512]{2,1,0:T(4,128)(2,1)S(1)} %get-tuple-element.204), channel_id=1, source_target_pairs={{0,4},{4,8},{8,12},{12,16},{16,20},{20,24},{24,28},{28,0},{1,5},{5... | collective-permute-start | bytes 221192 | tf_op jit(solution)/shard_map/ppermute | solution.py:26
  279.1 10.3 %collective-permute-start.25 = (bf16[24,3,512]{2,1,0:T(4,128)(2,1)S(1)}, bf16[24,3,512]{2,1,0:T(4,128)(2,1)S(1)}, u32[]{:S(2)}, u32[]{:S(2)}) collective-permute-start(bf16[24,3,512]{2,1,0:T(4,128)(2,1)S(1)} %get-tuple-element.205), channel_id=1, source_target_pairs={{4,0},{8,4},{12,8},{16,12},{20,16},{24,20},{28,24},{0,28},{5,1},{9... | collective-permute-start | bytes 221192 | tf_op jit(solution)/shard_map/ppermute | solution.py:28
  289.5 6.1 collective-permute-start.26
  290.8 4.8 collective-permute-start.27
  312.6 4.1 collective-permute-start.29
  314.2 6.8 collective-permute-start.28
  315.4 148.5 %reduce-scatter.9.cloned.1.call-start = ((), (), s32[]{:S(2)}) async-start(), calls=%async_computation.5 | async-start | bytes 61440 | tf_op jit(solution)/shard_map/reduce_scatter | solution.py:164
  321.7 293.4 %reduce-scatter.13.cloned.1.call-start = ((), (), s32[]{:S(2)}) async-start(), calls=%async_computation.8 | async-start | bytes 8650752
  339.0 423.0 %reduce-scatter.11.cloned.1.call-start = ((), (), s32[]{:S(2)}) async-start(), calls=%async_computation.6 | async-start | bytes 8650752 | tf_op jit(solution)/shard_map/reduce_scatter | solution.py:199
  349.7 115.0 %copy-start.16 = (f32[24,32,512]{2,1,0:T(8,128)S(1)}, f32[24,32,512]{2,1,0:T(8,128)}, u32[]{:S(2)}) copy-start(f32[24,32,512]{2,1,0:T(8,128)} %copy-done.15) | copy-start | bytes 4718596
  349.7 115.0 %copy-start.49 = (bf16[512,8]{0,1:T(8,128)(2,1)S(1)}, bf16[512,8]{0,1:T(8,128)(2,1)}, u32[]{:S(2)}) copy-start(bf16[512,8]{0,1:T(8,128)(2,1)} %param.38) | copy-start | bytes 24580
  616.0 147.6 %copy-start.1 = (bf16[512,2048]{1,0:T(8,128)(2,1)S(1)}, bf16[512,2048]{1,0:T(8,128)(2,1)}, u32[]{:S(2)}) copy-start(bf16[512,2048]{1,0:T(8,128)(2,1)} %param.34) | copy-start | bytes 6291460
  (267 other events, 1339.9 us)
Sparse Core Ops, SparseCore 0:
  233.1 19.3 reduce-scatter.6
  315.6 124.9 all-reduce.2
  443.6 20.2 reduce-scatter.8
  466.0 148.9 reduce-scatter.12
  617.2 144.7 reduce-scatter.10
where the time goes:
time: 780 us; the launch traced here: 771 us
  waiting for transfers between devices  463 us (59%)
  other arithmetic  128 us (16%)
  matrix products  54.6 us (7%)
  starting transfers between devices  52.4 us (7%)
  local copies, waits for them, and re-layouts  40 us (5%)
  between operations  19 us (2%)
  blocking collectives  13.6 us (2%)
    unnamed x6, waiting for transfers between devices  149 us
    reduce_scatter x1, waiting for transfers between devices, weight_sums(): lax.psum_scatter(jnp.concatenate(pieces, axis=1), ('wide', 'narrow'), sca...  144 us
    psum x1, waiting for transfers between devices, weight_sums(): kernel_sums = lax.psum(stacked, ('wide', 'narrow'))  90.8 us
    reduce_scatter x2, waiting for transfers between devices, remap_adjoint(): lax.psum_scatter(column.astype(jnp.bfloat16), 'narrow', scatter_dimension...  37.9 us
    ppermute x12, starting transfers between devices, extended(): lax.ppermute(head, axis, [((i + 1) % count, i) for i in range(ends)])  35 us
    dot_general x8, other arithmetic, block_backward(): jnp.einsum('rcd,rcd->d', d_taps, window, preferred_element_type=jnp.float32)  32 us
    reduce_sum x2, other arithmetic, block_forward(): center = mixed_taps - jnp.mean(mixed_taps, axis=-1, keepdims=True)  27.6 us
    ppermute x12, waiting for transfers between devices, extended(): lax.ppermute(tail, axis, [(i, (i + 1) % count) for i in range(ends)])  24.4 us
  transfers between devices with their start and end apart: 35, of which 21 were waited for; matrix products, arithmetic and copies ran while one was open for 10% of the time, Pallas kernels for 0%

commit v1 on v0

--- a/solution.py
+++ b/solution.py
@@ -11,8 +11,37 @@
 highest = lax.Precision.HIGHEST
 
 
-def from_partner(shard, axis, distance):
-    return lax.ppermute(shard, axis, [(i, i ^ 1 << distance) for i in range(lax.axis_size(axis))])
+def pairs_along(axis, bit):
+    return [(i, i ^ (1 << bit)) for i in range(lax.axis_size(axis))]
+
+
+def bits_of(axis):
+    return lax.axis_size(axis).bit_length() - 1
+
+
+def scatter_sum(partial, order):
+    labels = [("wide", bit) for bit in reversed(range(bits_of("wide")))]
+    labels += [("narrow", bit) for bit in reversed(range(bits_of("narrow")))]
+    rows, cols = partial.shape
+    running = partial.reshape((2,) * len(labels) + (rows >> len(labels), cols))
+    for axis, bit in order:
+        dim = labels.index((axis, bit))
+        labels.pop(dim)
+        mine = (lax.axis_index(axis) >> bit) & 1
+        keep = lax.dynamic_index_in_dim(running, mine, dim, keepdims=False)
+        away = lax.dynamic_index_in_dim(running, 1 - mine, dim, keepdims=False)
+        came = lax.ppermute(away, axis, pairs_along(axis, bit))
+        running = keep.astype(jnp.float32) + came.astype(jnp.float32)
+        if labels:
+            running = running.astype(jnp.bfloat16)
+    return running
+
+
+def full_sum(partial):
+    for axis in ("narrow", "wide"):
+        for bit in range(bits_of(axis)):
+            partial = partial + lax.ppermute(partial, axis, pairs_along(axis, bit))
+    return partial
 
 
 def extended(cells, sides, width, closed):
@@ -45,10 +74,9 @@
 
 
 def fold_rows(top_band):
-    levels = lax.axis_size("wide").bit_length() - 1
-    for bit_place in range(levels):
-        top_band = from_partner(top_band, "wide", bit_place)
-    return top_band[::-1, ::-1]
+    cols, rows = lax.axis_size("wide"), lax.axis_size("narrow")
+    pairs = [(w * rows + rows - 1, (cols - 1 - w) * rows + rows - 1) for w in range(cols)]
+    return lax.ppermute(top_band, ("wide", "narrow"), pairs)[::-1, ::-1]
 
 
 def extend(fields, folded):
@@ -131,40 +159,33 @@
     return (incoming + spread, (normed, d_before, hidden, flat_round, kernel_term))
 
 
-def remap_apply(fields, sources, targets, weights):
+def around(tile):
+    column = lax.all_gather(tile, "narrow", axis=0, tiled=False)
+    return extended(column[None], (("wide", 0),), 1, True)
+
+
+def remap_matrix(sources, targets, weights, block_count):
+    blocks = 3 * lax.axis_size("narrow") * block_count
+    placing = (targets[:, None] == jnp.arange(block_count)).astype(jnp.float32) * weights[:, None]
+    choose = (sources[:, None] == jnp.arange(blocks)).astype(jnp.float32)
+    return jnp.einsum("eb,es->bs", placing, choose, precision=highest)
+
+
+def adjoint_matrix(lists, block_count):
+    sources, targets, weights = lists
     lat_count = lax.axis_size("narrow")
-    block_count = fields.shape[0]
-    column = lax.all_gather(fields[None], "narrow", axis=0, tiled=True)
-    beside_all = extended(column, (("wide", 0),), lat_count, True)
-    flat_blocks = beside_all.reshape(-1, fields.shape[1], fields.shape[2])
-    picked = flat_blocks[sources].astype(jnp.float32)
-    placing = (targets[:, None] == jnp.arange(block_count, dtype=jnp.int32)[None, :]).astype(
-        jnp.float32
-    ) * weights[:, None]
-    return jnp.einsum("eb,ekp->bkp", placing, picked, precision=highest)
-
-
-def remap_adjoint(gradient, sources, targets, weights):
-    lat_count = lax.axis_size("narrow")
-    block_count = gradient.shape[0]
-    placing = (targets[:, None] == jnp.arange(block_count, dtype=jnp.int32)[None, :]).astype(
-        jnp.float32
-    ) * weights[:, None]
-    d_picked = jnp.einsum("eb,bkp->ekp", placing, gradient, precision=highest)
-    choose = (
-        sources[:, None] == jnp.arange(3 * lat_count * block_count, dtype=jnp.int32)[None, :]
-    ).astype(jnp.float32)
-    d_flat = jnp.einsum("ef,ekp->fkp", choose, d_picked, precision=highest)
-    d_flat = d_flat.reshape(3 * lat_count, block_count, gradient.shape[1], gradient.shape[2])
-    outward = jnp.concatenate([d_flat[:lat_count], d_flat[2 * lat_count :]], axis=0)
-    returned = extended(outward.astype(jnp.bfloat16), (("wide", 0),), lat_count, True).astype(
-        outward.dtype
-    )
-    column = d_flat[lat_count : 2 * lat_count] + returned[:lat_count] + returned[3 * lat_count :]
-    own_part = lax.psum_scatter(
-        column.astype(jnp.bfloat16), "narrow", scatter_dimension=0, tiled=True
-    ).astype(jnp.float32)
-    return own_part[0]
+    own = lax.axis_index("narrow")
+    offset = 2 - jnp.arange(3)
+    first = (offset[:, None, None] * lat_count + own) * block_count
+    local = (sources - first)[..., None]
+    choose = (local == jnp.arange(block_count)).astype(jnp.float32) * weights[..., None]
+    placing = (targets[..., None] == jnp.arange(block_count)).astype(jnp.float32)
+    return jnp.einsum("ones,oneb->sonb", choose, placing, precision=highest).reshape(block_count, -1)
+
+
+def remap(matrix, fields):
+    flat_blocks = around(fields).reshape(-1, fields.shape[1], fields.shape[2])
+    return jnp.einsum("bs,skp->bkp", matrix, flat_blocks.astype(jnp.float32), precision=highest)
 
 
 def to_cells(blocks, lift_weight, row_count, col_count):
@@ -186,37 +207,19 @@
     return spread.reshape(row_count, col_count, head_weight.shape[0])
 
 
-def weight_sums(records):
-    channels = records[0][0].shape[1]
-    hidden_units = records[0][2].shape[1]
-    stacked = jnp.stack([record[4] for record in records])
-    pieces = [
-        lax.dot_general(
-            record[0], record[1], (((0,), (0,)), ((), ())), preferred_element_type=jnp.float32
-        )
-        for record in records
-    ]
-    inner_sums = lax.psum_scatter(
-        jnp.concatenate(pieces, axis=1), ("wide", "narrow"), scatter_dimension=0, tiled=True
-    )
-    pieces = [
-        lax.dot_general(
-            record[2], record[3], (((0,), (0,)), ((), ())), preferred_element_type=jnp.float32
-        )
-        for record in records
-    ]
-    outer_sums = lax.psum_scatter(
-        jnp.concatenate(pieces, axis=1), ("wide", "narrow"), scatter_dimension=0, tiled=True
-    )
-    kernel_sums = lax.psum(stacked, ("wide", "narrow"))
-    results = []
-    for grid_index in range(len(records)):
-        inner_part = (
-            inner_sums[:, grid_index * hidden_units : (grid_index + 1) * hidden_units] / grad_scale
-        )
-        outer_part = outer_sums[:, grid_index * channels : (grid_index + 1) * channels] / grad_scale
-        results.append((inner_part, outer_part, kernel_sums[grid_index] / grad_scale))
-    return results
+def weight_sums(record):
+    normed, d_before, hidden, flat_round, _ = record
+    inner_part = lax.dot_general(
+        normed, d_before, (((0,), (0,)), ((), ())), preferred_element_type=jnp.float32
+    ).astype(jnp.bfloat16)
+    outer_part = lax.dot_general(
+        hidden, flat_round, (((0,), (0,)), ((), ())), preferred_element_type=jnp.float32
+    ).astype(jnp.bfloat16)
+    wide_bits = [("wide", bit) for bit in range(bits_of("wide"))]
+    narrow_bits = [("narrow", bit) for bit in range(bits_of("narrow"))]
+    one = narrow_bits + wide_bits
+    other = narrow_bits[:1] + wide_bits[:1] + narrow_bits[1:] + wide_bits[1:]
+    return scatter_sum(inner_part, one) / grad_scale, scatter_sum(outer_part, other) / grad_scale
 
 
 def per_device(
@@ -246,19 +249,26 @@
 ):
     row_count, col_count, channels = atmos_state.shape
     wet_cells = wet_mask.astype(jnp.float32)[:, :, None]
+    block_count = row_count * col_count // 128
     flux_lists = (flux_source.reshape(-1), flux_target.reshape(-1), flux_weight.reshape(-1))
     surface_lists = (
         surface_source.reshape(-1),
         surface_target.reshape(-1),
         surface_weight.reshape(-1),
     )
+    flux_matrix = remap_matrix(*flux_lists, block_count)
+    surface_matrix = remap_matrix(*surface_lists, block_count)
+    lists = jnp.stack([part.astype(jnp.float32) for part in flux_lists + surface_lists])
+    lists = jnp.moveaxis(around(lists), 2, 0)
+    flux_adjoint = adjoint_matrix(lists[:3], block_count)
+    surface_adjoint = adjoint_matrix(lists[3:], block_count)
     surface = jnp.einsum(
         "bpd,dk->bkp",
         ocean_state.reshape(-1, 128, channels),
         surface_head,
         preferred_element_type=jnp.float32,
     ).astype(jnp.bfloat16)
-    to_atmos = remap_apply(surface, surface_lists[0], surface_lists[1], surface_lists[2])
+    to_atmos = remap(surface_matrix, surface)
     atmos_start = (atmos_state + to_cells(to_atmos, surface_lift, row_count, col_count)).astype(
         jnp.bfloat16
     )
@@ -272,7 +282,7 @@
         flux_head,
         preferred_element_type=jnp.float32,
     ).astype(jnp.bfloat16)
-    to_ocean = remap_apply(fluxes, flux_lists[0], flux_lists[1], flux_lists[2])
+    to_ocean = remap(flux_matrix, fluxes)
     ocean_start = (
         (ocean_state + to_cells(to_ocean, flux_lift, row_count, col_count)) * wet_cells
     ).astype(jnp.bfloat16)
@@ -285,24 +295,19 @@
         ocean_stored, ocean_kernel, ocean_gain, ocean_inner, ocean_outer, ocean_total, True
     )
     ocean_start_grad = ocean_start_grad * wet_cells
-    flux_grad = remap_adjoint(
-        lift_back(ocean_start_grad, flux_lift), flux_lists[0], flux_lists[1], flux_lists[2]
-    )
+    flux_grad = remap(flux_adjoint, lift_back(ocean_start_grad, flux_lift).astype(jnp.bfloat16))
     atmos_total = atmos_cotangent + head_back(flux_grad, flux_head, row_count, col_count)
     atmos_start_grad, atmos_record = block_backward(
         atmos_stored, atmos_kernel, atmos_gain, atmos_inner, atmos_outer, atmos_total, False
     )
     atmos_state_grad = atmos_start_grad.astype(jnp.bfloat16)
-    surface_grad = remap_adjoint(
-        lift_back(atmos_start_grad, surface_lift),
-        surface_lists[0],
-        surface_lists[1],
-        surface_lists[2],
-    )
+    surface_grad = remap(surface_adjoint, lift_back(atmos_start_grad, surface_lift).astype(jnp.bfloat16))
     ocean_state_grad = (
         ocean_start_grad + head_back(surface_grad, surface_head, row_count, col_count)
     ).astype(jnp.bfloat16)
-    atmos_sums, ocean_sums = weight_sums([atmos_record, ocean_record])
+    ocean_sums = weight_sums(ocean_record)
+    atmos_sums = weight_sums(atmos_record)
+    kernel_sums = full_sum(jnp.stack([atmos_record[4], ocean_record[4]])) / grad_scale
     return (
         atmos_next,
         ocean_next,
@@ -310,10 +315,10 @@
         ocean_state_grad,
         atmos_sums[0],
         atmos_sums[1],
-        atmos_sums[2],
+        kernel_sums[0],
         ocean_sums[0],
         ocean_sums[1],
-        ocean_sums[2],
+        kernel_sums[1],
     )
 
 

time: 780 us -> 405 us (0.52)
  waiting for transfers between devices: 463 us -> 55.4 us
  starting transfers between devices: 52.4 us -> 100 us
  blocking collectives: 13.6 us -> 38.6 us
  other arithmetic: 128 us -> 114 us
  between operations: 19 us -> 5.72 us
    reduce_scatter x3 -> x0, waiting for transfers between devices: 182 us -> none  [the longest x1 144 us: weight_sums(): lax.psum_scatter(jnp.concatenate(pieces, axis=1), ('wide', 'narrow'), sca...]
    unnamed x6 -> x0, waiting for transfers between devices: 149 us -> none
    psum x1 -> x0, waiting for transfers between devices: 90.8 us -> none  [weight_sums(): kernel_sums = lax.psum(stacked, ('wide', 'narrow'))]
    ppermute x6 -> x27, starting transfers between devices: 2.7 us -> 34.9 us  [the longest x20 27.7 us: scatter_sum(): came = lax.ppermute(away, axis, pairs_along(axis, bit))]
    ppermute x6 -> x27, waiting for transfers between devices: 10.3 us -> 37.9 us  [the longest x20 21.3 us: scatter_sum(): came = lax.ppermute(away, axis, pairs_along(axis, bit))]
    all_gather x2 -> x5, blocking collectives: 13.6 us -> 38.6 us  [around(): column = lax.all_gather(tile, 'narrow', axis=0, tiled=False)]
    ppermute x12 -> x13, starting transfers between devices: 35 us -> 53.7 us  [extended(): lax.ppermute(head, axis, [((i + 1) % count, i) for i in range(ends)])]
    ppermute x12 -> x13, waiting for transfers between devices: 24.4 us -> 11.4 us  [extended(): lax.ppermute(tail, axis, [(i, (i + 1) % count) for i in range(ends)])]
  transfers between devices with their start and end apart: 35 -> 53, of which waited for: 21 -> 20; matrix products, arithmetic and copies ran while one was open for 10% -> 29% of each run, Pallas kernels for 0% -> 0%
where the time goes in v1:
time: 405 us; the launch traced here: 399 us
  other arithmetic  114 us (28%)
  starting transfers between devices  100 us (25%)
  waiting for transfers between devices  55.4 us (14%)
  matrix products  49.4 us (12%)
  blocking collectives  38.6 us (10%)
  local copies, waits for them, and re-layouts  35 us (9%)
  between operations  5.72 us (1%)
    ppermute x13, starting transfers between devices, extended(): lax.ppermute(head, axis, [((i + 1) % count, i) for i in range(ends)])  53.7 us
    all_gather x5, blocking collectives, around(): column = lax.all_gather(tile, 'narrow', axis=0, tiled=False)  38.6 us
    ppermute x20, starting transfers between devices, scatter_sum(): came = lax.ppermute(away, axis, pairs_along(axis, bit))  27.7 us
    dot_general x8, other arithmetic, block_backward(): jnp.einsum('rcd,rcd->d', d_taps, window, preferred_element_type=jnp.float32)  27.6 us
    reduce_sum x2, other arithmetic, block_forward(): center = mixed_taps - jnp.mean(mixed_taps, axis=-1, keepdims=True)  25.6 us
    ppermute x20, waiting for transfers between devices, scatter_sum(): came = lax.ppermute(away, axis, pairs_along(axis, bit))  21.3 us
    ppermute x5, waiting for transfers between devices, full_sum(): partial = partial + lax.ppermute(partial, axis, pairs_along(axis, bit))  16.6 us
    convert_element_type x1, other arithmetic, per_device(): atmos_state_grad = atmos_start_grad.astype(jnp.bfloat16)  14.1 us
  transfers between devices with their start and end apart: 53, of which 20 were waited for; matrix products, arithmetic and copies ran while one was open for 29% of the time, Pallas kernels for 0%

profile of v1, /device:TPU:0, one launch (start us, length us, event | category | flops | bytes accessed | tf_op | source)
XLA Modules:
  0.0 398.7 jit_solution(4509460280656203258)
XLA Ops:
  2.9 6.2 %all-gather.5 = f32[4,6,48]{2,1,0:T(8,128)S(1)} all-gather(f32[1,6,48]{2,1,0:T(8,128)S(1)} %bitcast.1139), channel_id=4, replica_groups=mesh['wide'=8,'narrow'=4] {'narrow'}, dimensions={0}, use_global_device_ids=true | all-gather | bytes 5760 | tf_op jit(solution)/shard_map/all_gather | solution.py:163
  9.1 4.9 %collective-permute-start.14 = (f32[1,4,6,48]{3,2,1,0:T(8,128)S(1)}, f32[1,4,6,48]{3,2,1,0:T(8,128)S(1)}, u32[]{:S(2)}, u32[]{:S(2)}) collective-permute-start(f32[1,4,6,48]{3,2,1,0:T(8,128)S(1)} %bitcast.889), channel_id=1, source_target_pairs={{4,0},{8,4},{12,8},{16,12},{20,16},{24,20},{28,24},{0,28},{5,1},{9... | collective-permute-start | bytes 13832 | tf_op jit(solution)/shard_map/ppermute | solution.py:57
  15.5 5.4 %all-gather = bf16[24,8,128]{2,1,0:T(8,128)(2,1)S(1)} all-gather(bf16[6,8,128]{2,1,0:T(8,128)(2,1)S(1)} %fusion.170), channel_id=2, replica_groups=mesh['wide'=8,'narrow'=4] {'narrow'}, dimensions={0}, use_global_device_ids=true | all-gather | bytes 61440 | tf_op jit(solution)/shard_map/all_gather | solution.py:163
  20.9 4.7 %collective-permute-start.1 = (bf16[1,4,6,8,128]{4,3,2,1,0:T(8,128)(2,1)S(1)}, bf16[1,4,6,8,128]{4,3,2,1,0:T(8,128)(2,1)S(1)}, u32[]{:S(2)}, u32[]{:S(2)}) collective-permute-start(bf16[1,4,6,8,128]{4,3,2,1,0:T(8,128)(2,1)S(1)} %bitcast.881), channel_id=1, source_target_pairs={{4,0},{8,4},{12,8},{16,12},{20,16},{24,20},{28,24},{0,28},{5,1},{9... | collective-permute-start | bytes 147464 | tf_op jit(solution)/shard_map/ppermute | solution.py:57
  40.0 4.8 %collective-permute-start.3 = (bf16[24,3,512]{2,1,0:T(4,128)(2,1)S(1)}, bf16[24,3,512]{2,1,0:T(4,128)(2,1)S(1)}, u32[]{:S(2)}, u32[]{:S(2)}) collective-permute-start(bf16[24,3,512]{2,1,0:T(4,128)(2,1)S(1)} %get-tuple-element.179), channel_id=1, source_target_pairs={{4,0},{8,4},{12,8},{16,12},{20,16},{24,20},{28,24},{0,28},{5,1},{9... | collective-permute-start | bytes 221192 | tf_op jit(solution)/shard_map/ppermute | solution.py:57
  45.3 2.1 collective-permute-done.2
  51.8 2.2 collective-permute-done.5
  54.0 2.6 maximum_maximum_fusion
  57.0 12.7 %fusion.275 = (f32[24,32]{1,0:T(8,128)S(1)}, f32[24,32,512]{2,1,0:T(8,128)S(1)}) fusion(f32[512]{0:T(512)S(1)} %bitcast.1059, bf16[27,38,512]{2,1,0:T(8,128)(2,1)S(1)} %get-tuple-element.169, f32[512]{0:T(512)S(1)} %bitcast.1061, f32[512]{0:T(512)S(1)} %bitcast.1065, f32[512]{0:T(512)S(1)} %bitcast.1067, f32[512]{0:T(512)S(1)} %bitcast.1069, ...), kind=kLoop, calls=%fused_computation.576 | loop fusion | flops 64879872 | bytes 35640320 | tf_op jit(solution)/shard_map/reduce_sum | solution.py:110
  72.0 4.3 %multiply_convert_fusion.1 = (bf16[768,2048]{1,0:T(8,128)(2,1)S(1)}, f32[768,2048]{1,0:T(8,128)}) fusion(bf16[768,512]{1,0:T(8,128)(2,1)S(1)} %bitcast.865, bf16[512,2048]{1,0:T(8,128)(2,1)S(1)} %copy-done.296), kind=kOutput, calls=%fused_computation.114 | convolution fusion | flops 1618477056 | bytes 12320768 | tf_op jit(solution)/shard_map/dot_general | solution.py:114
  79.0 7.5 %all-gather.1 = bf16[24,8,128]{2,1,0:T(8,128)(2,1)S(1)} all-gather(bf16[6,8,128]{2,1,0:T(8,128)(2,1)S(1)} %fusion.171), channel_id=3, replica_groups=mesh['wide'=8,'narrow'=4] {'narrow'}, dimensions={0}, use_global_device_ids=true | all-gather | bytes 61440 | tf_op jit(solution)/shard_map/all_gather | solution.py:163
  86.5 4.6 %collective-permute-start.7 = (bf16[1,4,6,8,128]{4,3,2,1,0:T(8,128)(2,1)S(1)}, bf16[1,4,6,8,128]{4,3,2,1,0:T(8,128)(2,1)S(1)}, u32[]{:S(2)}, u32[]{:S(2)}) collective-permute-start(bf16[1,4,6,8,128]{4,3,2,1,0:T(8,128)(2,1)S(1)} %bitcast.884), channel_id=1, source_target_pairs={{4,0},{8,4},{12,8},{16,12},{20,16},{24,20},{28,24},{0,28},{5,1},{9... | collective-permute-start | bytes 147464 | tf_op jit(solution)/shard_map/ppermute | solution.py:57
  92.9 5.0 %collective-permute-done.6 = bf16[1,4,6,8,128]{4,3,2,1,0:T(8,128)(2,1)S(1)} collective-permute-done((bf16[1,4,6,8,128]{4,3,2,1,0:T(8,128)(2,1)S(1)}, bf16[1,4,6,8,128]{4,3,2,1,0:T(8,128)(2,1)S(1)}, u32[]{:S(2)}, u32[]{:S(2)}) %collective-permute-start.6) | collective-permute-done | bytes 49184 | tf_op jit(solution)/shard_map/ppermute | solution.py:55
  100.4 13.3 %collective-permute-start.9 = (bf16[24,3,512]{2,1,0:T(4,128)(2,1)S(1)}, bf16[24,3,512]{2,1,0:T(4,128)(2,1)S(1)}, u32[]{:S(2)}, u32[]{:S(2)}) collective-permute-start(bf16[24,3,512]{2,1,0:T(4,128)(2,1)S(1)} %get-tuple-element.177), channel_id=1, source_target_pairs={{4,0},{8,4},{12,8},{16,12},{20,16},{24,20},{28,24},{0,28},{5,1},{9... | collective-permute-start | bytes 221192 | tf_op jit(solution)/shard_map/ppermute | solution.py:57
  113.8 2.1 collective-permute-done.9
  121.1 3.7 collective-permute-start.10
  124.8 2.8 rev.6
  128.9 2.7 maximum_maximum_fusion.1
  132.0 12.9 %fusion.273 = (f32[24,32]{1,0:T(8,128)S(1)}, f32[24,32,512]{2,1,0:T(8,128)S(1)}) fusion(f32[512]{0:T(512)S(1)} %bitcast.892, bf16[27,38,512]{2,1,0:T(8,128)(2,1)S(1)} %get-tuple-element.165, f32[512]{0:T(512)S(1)} %bitcast.895, f32[512]{0:T(512)S(1)} %bitcast.898, f32[512]{0:T(512)S(1)} %bitcast.901, f32[512]{0:T(512)S(1)} %bitcast.904, ...), kind=kLoop, calls=%fused_computation.575 | loop fusion | flops 64879872 | bytes 35640320 | tf_op jit(solution)/shard_map/reduce_sum | solution.py:110
  146.1 2.7 multiply_convert_fusion
  148.8 3.2 convolution_convert_fusion
  152.0 3.0 fusion.289
  155.0 3.9 fusion.5
  158.9 3.0 multiply_reduce_fusion.3
  161.9 2.5 multiply_reduce_fusion.2
  164.7 6.5 %fusion.166 = (f32[512]{0:T(512)}, f32[512]{0:T(512)}, f32[512]{0:T(512)}, f32[512]{0:T(512)}, f32[512]{0:T(512)}, /*index=5*/f32[512]{0:T(512)}, f32[512]{0:T(5...) fusion(bf16[27,38,512]{2,1,0:T(8,128)(2,1)S(1)} %copy-done.7, ...), kind=kLoop, calls=%fused_computation.282 | loop fusion | flops 24763392 | bytes 18139136 | tf_op jit(solution)/shard_map/rcd,rcd->d/dot_general | solution.py:141
  171.2 4.8 %fusion.138 = (f32[512]{0:T(512)}, f32[512]{0:T(512)}, f32[512]{0:T(512)}, f32[512]{0:T(512)}, f32[512]{0:T(512)}, /*index=5*/f32[512]{0:T(512)}, f32[512]{0:T(5...) fusion(bf16[24,32,512]{2,1,0:T(8,128)(2,1)S(1)} %get-tuple-elem, ...), kind=kLoop, calls=%fused_computation.254 | loop fusion | flops 21617664 | bytes 14979072 | tf_op jit(solution)/shard_map/rcd,rcd->d/dot_general | solution.py:141
  178.5 5.1 %collective-permute-start.16 = (bf16[24,3,512]{2,1,0:T(4,128)(2,1)S(1)}, bf16[24,3,512]{2,1,0:T(4,128)(2,1)S(1)}, u32[]{:S(2)}, u32[]{:S(2)}) collective-permute-start(bf16[24,3,512]{2,1,0:T(4,128)(2,1)S(1)} %get-tuple-element.174), channel_id=1, source_target_pairs={{4,0},{8,4},{12,8},{16,12},{20,16},{24,20},{28,24},{0,28},{5,1},{9... | collective-permute-start | bytes 221192 | tf_op jit(solution)/shard_map/ppermute | solution.py:57
  183.7 3.2 fusion.148
  186.9 3.2 convolution_convert_fusion.1
  195.7 3.0 collective-permute-start.19
  204.5 13.3 %multiply_add_fusion = f32[24,32,512]{2,1,0:T(8,128)S(1)} fusion(bf16[24,32,512]{2,1,0:T(8,128)(2,1)S(1)} %get-tuple-element.140, bf16[24,3,512]{2,1,0:T(4,128)(2,1)S(1)} %copy-done.51, bf16[24,3,512]{2,1,0:T(4,128)(2,1)S(1)} %copy-done.49, bf16[27,38,512]{2,1,0:T(8,128)(2,1)S(1)} %get-tuple-element.161, bf16[27,38,512]{2,1,0:T(8,128)(2,1)S(1)} %get-tuple-element.160, ...), kind=kLoop, calls=%fused_computation.289 | loop fusion | flops 64487424 | bytes 35637248 | tf_op jit(solution)/shard_map/add | solution.py:102
  221.2 12.7 %all-gather.3 = bf16[24,8,128]{2,1,0:T(8,128)(2,1)S(1)} all-gather(bf16[6,8,128]{2,1,0:T(8,128)(2,1)S(1)} %fusion.168), channel_id=5, replica_groups=mesh['wide'=8,'narrow'=4] {'narrow'}, dimensions={0}, use_global_device_ids=true | all-gather | bytes 61440 | tf_op jit(solution)/shard_map/all_gather | solution.py:163
  233.9 2.9 collective-permute-start.21
  239.5 2.3 stack.410
  241.9 2.4 copy.825
  246.8 3.3 convolution_convert_fusion.2
  250.1 3.9 fusion.11
  254.0 3.1 convolution_convert_fusion.3
  257.2 3.0 multiply_reduce_fusion.1
  260.2 2.0 multiply_reduce_fusion
  262.6 4.7 %fusion.117 = (f32[512]{0:T(512)S(1)}, f32[512]{0:T(512)S(1)}, f32[512]{0:T(512)S(1)}, f32[512]{0:T(512)S(1)}, f32[512]{0:T(512)S(1)}, /*index=5*/f32[512]{0:T(5...) fusion(bf16[27,38,512]{2,1,0:T(8,128)(2,1)S(1)} %get-tuple-elem, ...), kind=kLoop, calls=%fused_computation.233 | loop fusion | flops 24763392 | bytes 18139136 | tf_op jit(solution)/shard_map/rcd,rcd->d/dot_general | solution.py:141
  268.0 3.9 fusion.89
  272.6 4.9 %collective-permute-start.23 = (bf16[24,3,512]{2,1,0:T(4,128)(2,1)S(1)}, bf16[24,3,512]{2,1,0:T(4,128)(2,1)S(1)}, u32[]{:S(2)}, u32[]{:S(2)}) collective-permute-start(bf16[24,3,512]{2,1,0:T(4,128)(2,1)S(1)} %get-tuple-element.173), channel_id=1, source_target_pairs={{4,0},{8,4},{12,8},{16,12},{20,16},{24,20},{28,24},{0,28},{5,1},{9... | collective-permute-start | bytes 221192 | tf_op jit(solution)/shard_map/ppermute | solution.py:57
  277.5 2.6 fusion.99
  282.9 3.0 collective-permute-start.25
  288.7 14.1 %fusion.272 = (bf16[24,32,512]{2,1,0:T(8,128)(2,1)}, f32[24,32,512]{2,1,0:T(8,128)S(1)}) fusion(f32[512]{0:T(512)S(1)} %bitcast.1060, bf16[27,38,512]{2,1,0:T(8,128)(2,1)S(1)} %get-tuple-element.157, f32[512]{0:T(512)S(1)} %bitcast.1062, f32[512]{0:T(512)S(1)} %bitcast.1066, f32[512]{0:T(512)S(1)} %bitcast.1068, f32[512]{0:T(512)S(1)} %bitcast.1070, ...), kind=kLoop, calls=%fused_computation.574 | loop fusion | flops 66060288 | bytes 38782976 | tf_op jit(solution)/shard_map/convert_element_type | solution.py:303
  303.6 6.9 %all-gather.4 = bf16[24,8,128]{2,1,0:T(8,128)(2,1)S(1)} all-gather(bf16[6,8,128]{2,1,0:T(8,128)(2,1)S(1)} %fusion.169), channel_id=6, replica_groups=mesh['wide'=8,'narrow'=4] {'narrow'}, dimensions={0}, use_global_device_ids=true | all-gather | bytes 61440 | tf_op jit(solution)/shard_map/all_gather | solution.py:163
  310.5 3.3 collective-permute-start.27
  313.9 2.1 collective-permute-start.39
  317.5 3.3 collective-permute-done.26
  322.7 6.5 %collective-permute-done.40 = f32[2,7,7,512]{3,2,1,0:T(8,128)S(1)} collective-permute-done((f32[2,7,7,512]{3,2,1,0:T(8,128)S(1)}, f32[2,7,7,512]{3,2,1,0:T(8,128)S(1)}, u32[]{:S(2)}, u32[]{:S(2)}) %collective-permute-start.40) | collective-permute-done | bytes 200736 | tf_op jit(solution)/shard_map/ppermute | solution.py:43
  330.5 5.3 %collective-permute-done.41 = f32[2,7,7,512]{3,2,1,0:T(8,128)S(1)} collective-permute-done((f32[2,7,7,512]{3,2,1,0:T(8,128)S(1)}, f32[2,7,7,512]{3,2,1,0:T(8,128)S(1)}, u32[]{:S(2)}, u32[]{:S(2)}) %collective-permute-start.41) | collective-permute-done | bytes 200736 | tf_op jit(solution)/shard_map/ppermute | solution.py:43
  343.3 4.1 %collective-permute-done.42 = f32[2,7,7,512]{3,2,1,0:T(8,128)S(1)} collective-permute-done((f32[2,7,7,512]{3,2,1,0:T(8,128)S(1)}, f32[2,7,7,512]{3,2,1,0:T(8,128)S(1)}, u32[]{:S(2)}, u32[]{:S(2)}) %collective-permute-start.42) | collective-permute-done | bytes 200736 | tf_op jit(solution)/shard_map/ppermute | solution.py:43
  349.9 2.6 collective-permute-start.29
  354.2 9.2 %collective-permute-done.34 = bf16[2,2,2,64,512]{4,3,0,1,2:T(8,128)(2,1)S(1)} collective-permute-done((bf16[2,2,2,64,512]{4,3,0,1,2:T(8,128)(2,1)S(1)}, bf16[2,2,2,64,512]{4,3,0,1,2:T(8,128)(2,1)S(1)}, u32[]{:S(2)}, u32[]{:S(2)}) %collective-permute-start.34) | collective-permute-done | bytes 524320 | tf_op jit(solution)/shard_map/ppermute | solution.py:33
  363.5 2.6 collective-permute-start.35
  371.0 3.0 collective-permute-start.51
  374.7 2.0 collective-permute-start.47
  377.4 2.8 collective-permute-start.52
  383.6 2.4 collective-permute-start.36
  386.1 3.1 collective-permute-done.36
  389.3 2.6 collective-permute-start.37
  395.2 2.7 collective-permute-done.32
  (813 shorter events, 98.0 us)
Async XLA Ops:
  0.6 145.4 %copy-start = (bf16[512,2048]{1,0:T(8,128)(2,1)S(1)}, bf16[512,2048]{1,0:T(8,128)(2,1)}, u32[]{:S(2)}) copy-start(bf16[512,2048]{1,0:T(8,128)(2,1)} %param.34) | copy-start | bytes 6291460
  0.7 36.6 %copy-start.292 = (s32[1,1,48]{2,1,0:T(1,128)S(1)}, s32[1,1,48]{2,1,0:T(1,128)}, u32[]{:S(2)}) copy-start(s32[1,1,48]{2,1,0:T(1,128)} %param.41) | copy-start | bytes 580
  0.7 36.6 %copy-start.291 = (s32[1,1,48]{2,1,0:T(1,128)S(1)}, s32[1,1,48]{2,1,0:T(1,128)}, u32[]{:S(2)}) copy-start(s32[1,1,48]{2,1,0:T(1,128)} %param.40) | copy-start | bytes 580
  0.7 36.6 %copy-start.289 = (f32[1,1,48]{2,1,0:T(1,128)S(1)}, f32[1,1,48]{2,1,0:T(1,128)}, u32[]{:S(2)}) copy-start(f32[1,1,48]{2,1,0:T(1,128)} %param.42) | copy-start | bytes 580
  0.7 37.7 %copy-start.61 = (bf16[8,512]{1,0:T(8,128)(2,1)S(1)}, bf16[8,512]{1,0:T(8,128)(2,1)}, u32[]{:S(2)}) copy-start(bf16[8,512]{1,0:T(8,128)(2,1)} %param.39) | copy-start | bytes 24580
  9.1 41.6 %collective-permute-start.14 = (f32[1,4,6,48]{3,2,1,0:T(8,128)S(1)}, f32[1,4,6,48]{3,2,1,0:T(8,128)S(1)}, u32[]{:S(2)}, u32[]{:S(2)}) collective-permute-start(f32[1,4,6,48]{3,2,1,0:T(8,128)S(1)} %bitcast.889), channel_id=1, source_target_pairs={{4,0},{8,4},{12,8},{16,12},{20,16},{24,20},{28,24},{0,28},{5,1},{9... | collective-permute-start | bytes 13832 | tf_op jit(solution)/shard_map/ppermute | solution.py:57
  14.0 36.6 %collective-permute-start.13 = (f32[1,4,6,48]{3,2,1,0:T(8,128)S(1)}, f32[1,4,6,48]{3,2,1,0:T(8,128)S(1)}, u32[]{:S(2)}, u32[]{:S(2)}) collective-permute-start(f32[1,4,6,48]{3,2,1,0:T(8,128)S(1)} %bitcast.890), channel_id=1, source_target_pairs={{0,4},{4,8},{8,12},{12,16},{16,20},{20,24},{24,28},{28,0},{1,5},{5... | collective-permute-start | bytes 13832 | tf_op jit(solution)/shard_map/ppermute | solution.py:55
  20.9 17.3 %collective-permute-start.1 = (bf16[1,4,6,8,128]{4,3,2,1,0:T(8,128)(2,1)S(1)}, bf16[1,4,6,8,128]{4,3,2,1,0:T(8,128)(2,1)S(1)}, u32[]{:S(2)}, u32[]{:S(2)}) collective-permute-start(bf16[1,4,6,8,128]{4,3,2,1,0:T(8,128)(2,1)S(1)} %bitcast.881), channel_id=1, source_target_pairs={{4,0},{8,4},{12,8},{16,12},{20,16},{24,20},{28,24},{0,28},{5,1},{9... | collective-permute-start | bytes 147464 | tf_op jit(solution)/shard_map/ppermute | solution.py:57
  25.6 12.6 %collective-permute-start = (bf16[1,4,6,8,128]{4,3,2,1,0:T(8,128)(2,1)S(1)}, bf16[1,4,6,8,128]{4,3,2,1,0:T(8,128)(2,1)S(1)}, u32[]{:S(2)}, u32[]{:S(2)}) collective-permute-start(bf16[1,4,6,8,128]{4,3,2,1,0:T(8,128)(2,1)S(1)} %bitcast.882), channel_id=1, source_target_pairs={{0,4},{4,8},{8,12},{12,16},{16,20},{20,24},{24,28},{28,0},{1,5},{5... | collective-permute-start | bytes 147464 | tf_op jit(solution)/shard_map/ppermute | solution.py:55
  27.1 29.5 %copy-start.167 = (f32[1,1,512]{2,1,0:T(1,128)}, f32[1,1,512]{2,1,0:T(1,128)S(1)}, u32[]{:S(2)}) copy-start(f32[1,1,512]{2,1,0:T(1,128)S(1)} %get-tuple-element.272) | copy-start | bytes 6148
  27.1 29.5 %copy-start.169 = (f32[1,1,512]{2,1,0:T(1,128)}, f32[1,1,512]{2,1,0:T(1,128)S(1)}, u32[]{:S(2)}) copy-start(f32[1,1,512]{2,1,0:T(1,128)S(1)} %get-tuple-element.273) | copy-start | bytes 6148
  27.1 29.5 %copy-start.171 = (f32[1,1,512]{2,1,0:T(1,128)}, f32[1,1,512]{2,1,0:T(1,128)S(1)}, u32[]{:S(2)}) copy-start(f32[1,1,512]{2,1,0:T(1,128)S(1)} %get-tuple-element.274) | copy-start | bytes 6148
  27.1 29.5 %copy-start.173 = (f32[1,1,512]{2,1,0:T(1,128)}, f32[1,1,512]{2,1,0:T(1,128)S(1)}, u32[]{:S(2)}) copy-start(f32[1,1,512]{2,1,0:T(1,128)S(1)} %get-tuple-element.275) | copy-start | bytes 6148
  32.2 99.4 %copy-start.64 = (f32[1,1,512]{2,1,0:T(1,128)}, f32[1,1,512]{2,1,0:T(1,128)S(1)}, u32[]{:S(2)}) copy-start(f32[1,1,512]{2,1,0:T(1,128)S(1)} %get-tuple-element.231) | copy-start | bytes 6148
  39.9 7.5 %collective-permute-start.2 = (bf16[24,3,512]{2,1,0:T(4,128)(2,1)S(1)}, bf16[24,3,512]{2,1,0:T(4,128)(2,1)S(1)}, u32[]{:S(2)}, u32[]{:S(2)}) collective-permute-start(bf16[24,3,512]{2,1,0:T(4,128)(2,1)S(1)} %get-tuple-element.178), channel_id=1, source_target_pairs={{0,4},{4,8},{8,12},{12,16},{16,20},{20,24},{24,28},{28,0},{1,5},{5... | collective-permute-start | bytes 221192 | tf_op jit(solution)/shard_map/ppermute | solution.py:55
  40.0 7.4 %collective-permute-start.3 = (bf16[24,3,512]{2,1,0:T(4,128)(2,1)S(1)}, bf16[24,3,512]{2,1,0:T(4,128)(2,1)S(1)}, u32[]{:S(2)}, u32[]{:S(2)}) collective-permute-start(bf16[24,3,512]{2,1,0:T(4,128)(2,1)S(1)} %get-tuple-element.179), channel_id=1, source_target_pairs={{4,0},{8,4},{12,8},{16,12},{20,16},{24,20},{28,24},{0,28},{5,1},{9... | collective-permute-start | bytes 221192 | tf_op jit(solution)/shard_map/ppermute | solution.py:57
  47.5 3.6 collective-permute-start.4
  48.8 5.1 %collective-permute-start.5 = (bf16[3,38,512]{2,1,0:T(8,128)(2,1)S(1)}, bf16[3,38,512]{2,1,0:T(8,128)(2,1)}, u32[]{:S(2)}, u32[]{:S(2)}) collective-permute-start(bf16[3,38,512]{2,1,0:T(8,128)(2,1)S(1)} %get-tuple-element.171), channel_id=1, source_target_pairs={{1,0},{2,1},{3,2},{5,4},{6,5},{7,6},{9,8},{10,9},{11,10},{13,12},{... | collective-permute-start | bytes 350216 | tf_op jit(solution)/shard_map/ppermute | solution.py:57
  50.7 48.3 %copy-start.56 = (f32[24,32]{1,0:T(8,128)}, f32[24,32]{1,0:T(8,128)S(1)}, u32[]{:S(2)}) copy-start(f32[24,32]{1,0:T(8,128)S(1)} %convert_element_type.1134) | copy-start | bytes 9220
  86.5 6.4 %collective-permute-start.7 = (bf16[1,4,6,8,128]{4,3,2,1,0:T(8,128)(2,1)S(1)}, bf16[1,4,6,8,128]{4,3,2,1,0:T(8,128)(2,1)S(1)}, u32[]{:S(2)}, u32[]{:S(2)}) collective-permute-start(bf16[1,4,6,8,128]{4,3,2,1,0:T(8,128)(2,1)S(1)} %bitcast.884), channel_id=1, source_target_pairs={{4,0},{8,4},{12,8},{16,12},{20,16},{24,20},{28,24},{0,28},{5,1},{9... | collective-permute-start | bytes 147464 | tf_op jit(solution)/shard_map/ppermute | solution.py:57
  91.1 6.8 %collective-permute-start.6 = (bf16[1,4,6,8,128]{4,3,2,1,0:T(8,128)(2,1)S(1)}, bf16[1,4,6,8,128]{4,3,2,1,0:T(8,128)(2,1)S(1)}, u32[]{:S(2)}, u32[]{:S(2)}) collective-permute-start(bf16[1,4,6,8,128]{4,3,2,1,0:T(8,128)(2,1)S(1)} %bitcast.885), channel_id=1, source_target_pairs={{0,4},{4,8},{8,12},{12,16},{16,20},{20,24},{24,28},{28,0},{1,5},{5... | collective-permute-start | bytes 147464 | tf_op jit(solution)/shard_map/ppermute | solution.py:55
  100.4 13.5 %collective-permute-start.8 = (bf16[24,3,512]{2,1,0:T(4,128)(2,1)S(1)}, bf16[24,3,512]{2,1,0:T(4,128)(2,1)S(1)}, u32[]{:S(2)}, u32[]{:S(2)}) collective-permute-start(bf16[24,3,512]{2,1,0:T(4,128)(2,1)S(1)} %get-tuple-element.176), channel_id=1, source_target_pairs={{0,4},{4,8},{8,12},{12,16},{16,20},{20,24},{24,28},{28,0},{1,5},{5... | collective-permute-start | bytes 221192 | tf_op jit(solution)/shard_map/ppermute | solution.py:55
  100.4 15.5 %collective-permute-start.9 = (bf16[24,3,512]{2,1,0:T(4,128)(2,1)S(1)}, bf16[24,3,512]{2,1,0:T(4,128)(2,1)S(1)}, u32[]{:S(2)}, u32[]{:S(2)}) collective-permute-start(bf16[24,3,512]{2,1,0:T(4,128)(2,1)S(1)} %get-tuple-element.177), channel_id=1, source_target_pairs={{4,0},{8,4},{12,8},{16,12},{20,16},{24,20},{28,24},{0,28},{5,1},{9... | collective-permute-start | bytes 221192 | tf_op jit(solution)/shard_map/ppermute | solution.py:57
  116.8 10.8 %collective-permute-start.12 = (bf16[3,38,512]{2,1,0:T(8,128)(2,1)}, bf16[3,38,512]{2,1,0:T(8,128)(2,1)}, u32[]{:S(2)}, u32[]{:S(2)}) collective-permute-start(bf16[3,38,512]{2,1,0:T(8,128)(2,1)} %get-tuple-element.166), channel_id=1, source_target_pairs={{1,0},{2,1},{3,2},{5,4},{6,5},{7,6},{9,8},{10,9},{11,10},{13,12},{... | collective-permute-start | bytes 350216 | tf_op jit(solution)/shard_map/ppermute | solution.py:57
  118.0 6.7 %collective-permute-start.11 = (bf16[3,38,512]{2,1,0:T(8,128)(2,1)}, bf16[3,38,512]{2,1,0:T(8,128)(2,1)}, u32[]{:S(2)}, u32[]{:S(2)}) collective-permute-start(bf16[3,38,512]{2,1,0:T(8,128)(2,1)} %get-tuple-element.167), channel_id=1, source_target_pairs={{3,31},{7,27},{11,23},{15,19},{19,15},{23,11},{27,7},{31,3}} | collective-permute-start | bytes 350216 | tf_op jit(solution)/shard_map/ppermute | solution.py:79
  121.1 7.8 %collective-permute-start.10 = (bf16[3,38,512]{2,1,0:T(8,128)(2,1)}, bf16[3,38,512]{2,1,0:T(8,128)(2,1)}, u32[]{:S(2)}, u32[]{:S(2)}) collective-permute-start(bf16[3,38,512]{2,1,0:T(8,128)(2,1)} %get-tuple-element.167), channel_id=1, source_target_pairs={{0,1},{1,2},{2,3},{4,5},{5,6},{6,7},{8,9},{9,10},{10,11},{12,13},{... | collective-permute-start | bytes 350216 | tf_op jit(solution)/shard_map/ppermute | solution.py:55
  178.3 158.6 %collective-permute-start.48 = (bf16[2,2,2,2,64,512]{5,4,0,1,3,2:T(8,128)(2,1)}, bf16[2,2,2,2,64,512]{5,4,0,1,3,2:T(8,128)(2,1)}, u32[]{:S(2)}, u32[]{:S(2)}) collective-permute-start(bf16[2,2,2,2,64,512]{5,4,0,1,3,2:T(8,128)(2,1)} %bitcast.846), channel_id=1, source_target_pairs={{0,1},{1,0},{2,3},{3,2},{4,5},{5,4},{6,7},{7,6},{8,9},{9,8},{10,11... | collective-permute-start | bytes 3145736 | tf_op jit(solution)/shard_map/ppermute | solution.py:33
  178.5 11.5 %collective-permute-start.16 = (bf16[24,3,512]{2,1,0:T(4,128)(2,1)S(1)}, bf16[24,3,512]{2,1,0:T(4,128)(2,1)S(1)}, u32[]{:S(2)}, u32[]{:S(2)}) collective-permute-start(bf16[24,3,512]{2,1,0:T(4,128)(2,1)S(1)} %get-tuple-element.174), channel_id=1, source_target_pairs={{4,0},{8,4},{12,8},{16,12},{20,16},{24,20},{28,24},{0,28},{5,1},{9... | collective-permute-start | bytes 221192 | tf_op jit(solution)/shard_map/ppermute | solution.py:57
  183.6 7.4 %collective-permute-start.15 = (bf16[24,3,512]{2,1,0:T(4,128)(2,1)S(1)}, bf16[24,3,512]{2,1,0:T(4,128)(2,1)S(1)}, u32[]{:S(2)}, u32[]{:S(2)}) collective-permute-start(bf16[24,3,512]{2,1,0:T(4,128)(2,1)S(1)} %get-tuple-element.175), channel_id=1, source_target_pairs={{0,4},{4,8},{8,12},{12,16},{16,20},{20,24},{24,28},{28,0},{1,5},{5... | collective-permute-start | bytes 221192 | tf_op jit(solution)/shard_map/ppermute | solution.py:55
  191.8 8.6 %collective-permute-start.18 = (bf16[3,38,512]{2,1,0:T(8,128)(2,1)}, bf16[3,38,512]{2,1,0:T(8,128)(2,1)}, u32[]{:S(2)}, u32[]{:S(2)}) collective-permute-start(bf16[3,38,512]{2,1,0:T(8,128)(2,1)} %get-tuple-element.162), channel_id=1, source_target_pairs={{1,0},{2,1},{3,2},{5,4},{6,5},{7,6},{9,8},{10,9},{11,10},{13,12},{... | collective-permute-start | bytes 350216 | tf_op jit(solution)/shard_map/ppermute | solution.py:57
  193.1 5.6 %collective-permute-start.17 = (bf16[3,38,512]{2,1,0:T(8,128)(2,1)}, bf16[3,38,512]{2,1,0:T(8,128)(2,1)}, u32[]{:S(2)}, u32[]{:S(2)}) collective-permute-start(bf16[3,38,512]{2,1,0:T(8,128)(2,1)} %get-tuple-element.163), channel_id=1, source_target_pairs={{3,31},{7,27},{11,23},{15,19},{19,15},{23,11},{27,7},{31,3}} | collective-permute-start | bytes 350216 | tf_op jit(solution)/shard_map/ppermute | solution.py:79
  195.7 5.7 %collective-permute-start.19 = (bf16[3,38,512]{2,1,0:T(8,128)(2,1)}, bf16[3,38,512]{2,1,0:T(8,128)(2,1)S(1)}, u32[]{:S(2)}, u32[]{:S(2)}) collective-permute-start(bf16[3,38,512]{2,1,0:T(8,128)(2,1)} %get-tuple-element.163), channel_id=1, source_target_pairs={{0,1},{1,2},{2,3},{4,5},{5,6},{6,7},{8,9},{9,10},{10,11},{12,13},{... | collective-permute-start | bytes 350216 | tf_op jit(solution)/shard_map/ppermute | solution.py:55
  233.9 10.4 %collective-permute-start.21 = (bf16[1,4,6,8,128]{4,2,1,3,0:T(8,128)(2,1)S(1)}, bf16[1,4,6,8,128]{4,2,1,3,0:T(8,128)(2,1)S(1)}, u32[]{:S(2)}, u32[]{:S(2)}) collective-permute-start(bf16[1,4,6,8,128]{4,2,1,3,0:T(8,128)(2,1)S(1)} %copy.79), channel_id=1, source_target_pairs={{4,0},{8,4},{12,8},{16,12},{20,16},{24,20},{28,24},{0,28},{5,1},{9... | collective-permute-start | bytes 147464 | tf_op jit(solution)/shard_map/ppermute | solution.py:57
  236.8 7.5 %collective-permute-start.20 = (bf16[1,4,6,8,128]{4,2,1,3,0:T(8,128)(2,1)S(1)}, bf16[1,4,6,8,128]{4,2,1,3,0:T(8,128)(2,1)S(1)}, u32[]{:S(2)}, u32[]{:S(2)}) collective-permute-start(bf16[1,4,6,8,128]{4,2,1,3,0:T(8,128)(2,1)S(1)} %copy.79), channel_id=1, source_target_pairs={{0,4},{4,8},{8,12},{12,16},{16,20},{20,24},{24,28},{28,0},{1,5},{5... | collective-permute-start | bytes 147464 | tf_op jit(solution)/shard_map/ppermute | solution.py:55
  244.3 95.8 %collective-permute-start.43 = (bf16[2,2,2,2,16,2048]{5,4,0,1,2,3:T(8,128)(2,1)}, bf16[2,2,2,2,16,2048]{5,4,0,1,2,3:T(8,128)(2,1)}, u32[]{:S(2)}, u32[]{:S(2)}) collective-permute-start(bf16[2,2,2,2,16,2048]{5,4,0,1,2,3:T(8,128)(2,1)} %bitcast.847), channel_id=1, source_target_pairs={{0,1},{1,0},{2,3},{3,2},{4,5},{5,4},{6,7},{7,6},{8,9},{9,8},{10,11... | collective-permute-start | bytes 3145736 | tf_op jit(solution)/shard_map/ppermute | solution.py:33
  272.6 8.9 %collective-permute-start.22 = (bf16[24,3,512]{2,1,0:T(4,128)(2,1)}, bf16[24,3,512]{2,1,0:T(4,128)(2,1)S(1)}, u32[]{:S(2)}, u32[]{:S(2)}) collective-permute-start(bf16[24,3,512]{2,1,0:T(4,128)(2,1)} %get-tuple-element.172), channel_id=1, source_target_pairs={{0,4},{4,8},{8,12},{12,16},{16,20},{20,24},{24,28},{28,0},{1,5},{5... | collective-permute-start | bytes 221192 | tf_op jit(solution)/shard_map/ppermute | solution.py:55
  272.6 8.9 %collective-permute-start.23 = (bf16[24,3,512]{2,1,0:T(4,128)(2,1)S(1)}, bf16[24,3,512]{2,1,0:T(4,128)(2,1)S(1)}, u32[]{:S(2)}, u32[]{:S(2)}) collective-permute-start(bf16[24,3,512]{2,1,0:T(4,128)(2,1)S(1)} %get-tuple-element.173), channel_id=1, source_target_pairs={{4,0},{8,4},{12,8},{16,12},{20,16},{24,20},{28,24},{0,28},{5,1},{9... | collective-permute-start | bytes 221192 | tf_op jit(solution)/shard_map/ppermute | solution.py:57
  281.6 6.2 %collective-permute-start.24 = (bf16[3,38,512]{2,1,0:T(8,128)(2,1)S(1)}, bf16[3,38,512]{2,1,0:T(8,128)(2,1)S(1)}, u32[]{:S(2)}, u32[]{:S(2)}) collective-permute-start(bf16[3,38,512]{2,1,0:T(8,128)(2,1)S(1)} %get-tuple-element.158), channel_id=1, source_target_pairs={{1,0},{2,1},{3,2},{5,4},{6,5},{7,6},{9,8},{10,9},{11,10},{13,12},{... | collective-permute-start | bytes 350216 | tf_op jit(solution)/shard_map/ppermute | solution.py:57
  282.9 4.9 %collective-permute-start.25 = (bf16[3,38,512]{2,1,0:T(8,128)(2,1)S(1)}, bf16[3,38,512]{2,1,0:T(8,128)(2,1)S(1)}, u32[]{:S(2)}, u32[]{:S(2)}) collective-permute-start(bf16[3,38,512]{2,1,0:T(8,128)(2,1)S(1)} %get-tuple-element.159), channel_id=1, source_target_pairs={{0,1},{1,2},{2,3},{4,5},{5,6},{6,7},{8,9},{9,10},{10,11},{12,13},{... | collective-permute-start | bytes 350216 | tf_op jit(solution)/shard_map/ppermute | solution.py:55
  286.4 27.5 %collective-permute-start.38 = (f32[2,7,7,512]{3,2,1,0:T(8,128)S(1)}, f32[2,7,7,512]{3,2,1,0:T(8,128)S(1)}, u32[]{:S(2)}, u32[]{:S(2)}) collective-permute-start(f32[2,7,7,512]{3,2,1,0:T(8,128)S(1)} %constant_dynamic-update-slice_fusion), channel_id=1, source_target_pairs={{0,1},{1,0},{2,3},{3,2},{4,5},{5,4},{6,7},{7,6},{8,9},{9,8},{10,11... | collective-permute-start | bytes 602120 | tf_op jit(solution)/shard_map/ppermute | solution.py:43
  310.5 6.9 %collective-permute-start.27 = (bf16[1,4,6,8,128]{4,2,1,3,0:T(8,128)(2,1)S(1)}, bf16[1,4,6,8,128]{4,2,1,3,0:T(8,128)(2,1)S(1)}, u32[]{:S(2)}, u32[]{:S(2)}) collective-permute-start(bf16[1,4,6,8,128]{4,2,1,3,0:T(8,128)(2,1)S(1)} %copy.84), channel_id=1, source_target_pairs={{4,0},{8,4},{12,8},{16,12},{20,16},{24,20},{28,24},{0,28},{5,1},{9... | collective-permute-start | bytes 147464 | tf_op jit(solution)/shard_map/ppermute | solution.py:57
  313.8 7.0 %collective-permute-start.26 = (bf16[1,4,6,8,128]{4,2,1,3,0:T(8,128)(2,1)S(1)}, bf16[1,4,6,8,128]{4,2,1,3,0:T(8,128)(2,1)S(1)}, u32[]{:S(2)}, u32[]{:S(2)}) collective-permute-start(bf16[1,4,6,8,128]{4,2,1,3,0:T(8,128)(2,1)S(1)} %copy.84), channel_id=1, source_target_pairs={{0,4},{4,8},{8,12},{12,16},{16,20},{20,24},{24,28},{28,0},{1,5},{5... | collective-permute-start | bytes 147464 | tf_op jit(solution)/shard_map/ppermute | solution.py:55
  313.9 7.9 %collective-permute-start.39 = (f32[2,7,7,512]{3,2,1,0:T(8,128)S(1)}, f32[2,7,7,512]{3,2,1,0:T(8,128)S(1)}, u32[]{:S(2)}, u32[]{:S(2)}) collective-permute-start(f32[2,7,7,512]{3,2,1,0:T(8,128)S(1)} %add.1250), channel_id=1, source_target_pairs={{0,2},{1,3},{2,0},{3,1},{4,6},{5,7},{6,4},{7,5},{8,10},{9,11},{10,... | collective-permute-start | bytes 602120 | tf_op jit(solution)/shard_map/ppermute | solution.py:43
  317.4 30.7 %collective-permute-start.33 = (bf16[2,2,2,2,64,512]{5,4,0,1,3,2:T(8,128)(2,1)S(1)}, bf16[2,2,2,2,64,512]{5,4,0,1,3,2:T(8,128)(2,1)S(1)}, u32[]{:S(2)}, u32[]{:S(2)}) collective-permute-start(bf16[2,2,2,2,64,512]{5,4,0,1,3,2:T(8,128)(2,1)S(1)} %bitcast.874), channel_id=1, source_target_pairs={{0,1},{1,0},{2,3},{3,2},{4,5},{5,4},{6,7},{7,6},{8,9},{9,8},{10,11... | collective-permute-start | bytes 3145736 | tf_op jit(solution)/shard_map/ppermute | solution.py:33
  320.8 28.7 %collective-permute-start.28 = (bf16[2,2,2,2,16,2048]{5,4,0,1,2,3:T(8,128)(2,1)S(1)}, bf16[2,2,2,2,16,2048]{5,4,0,1,2,3:T(8,128)(2,1)S(1)}, u32[]{:S(2)}, u32[]{:S(2)}) collective-permute-start(bf16[2,2,2,2,16,2048]{5,4,0,1,2,3:T(8,128)(2,1)S(1)} %bitcast.873), channel_id=1, source_target_pairs={{0,1},{1,0},{2,3},{3,2},{4,5},{5,4},{6,7},{7,6},{8,9},{9,8},{10,11... | collective-permute-start | bytes 3145736 | tf_op jit(solution)/shard_map/ppermute | solution.py:33
  321.8 7.4 %collective-permute-start.40 = (f32[2,7,7,512]{3,2,1,0:T(8,128)S(1)}, f32[2,7,7,512]{3,2,1,0:T(8,128)S(1)}, u32[]{:S(2)}, u32[]{:S(2)}) collective-permute-start(f32[2,7,7,512]{3,2,1,0:T(8,128)S(1)} %add.1251), channel_id=1, source_target_pairs={{0,4},{4,0},{8,12},{12,8},{16,20},{20,16},{24,28},{28,24},{1,5},{5... | collective-permute-start | bytes 602120 | tf_op jit(solution)/shard_map/ppermute | solution.py:43
  329.3 6.6 %collective-permute-start.41 = (f32[2,7,7,512]{3,2,1,0:T(8,128)S(1)}, f32[2,7,7,512]{3,2,1,0:T(8,128)S(1)}, u32[]{:S(2)}, u32[]{:S(2)}) collective-permute-start(f32[2,7,7,512]{3,2,1,0:T(8,128)S(1)} %add.1252), channel_id=1, source_target_pairs={{0,8},{4,12},{8,0},{12,4},{16,24},{20,28},{24,16},{28,20},{1,9},{5... | collective-permute-start | bytes 602120 | tf_op jit(solution)/shard_map/ppermute | solution.py:43
  335.9 11.5 %collective-permute-start.42 = (f32[2,7,7,512]{3,2,1,0:T(8,128)S(1)}, f32[2,7,7,512]{3,2,1,0:T(8,128)S(1)}, u32[]{:S(2)}, u32[]{:S(2)}) collective-permute-start(f32[2,7,7,512]{3,2,1,0:T(8,128)S(1)} %add.1253), channel_id=1, source_target_pairs={{0,16},{4,20},{8,24},{12,28},{16,0},{20,4},{24,8},{28,12},{1,17},{... | collective-permute-start | bytes 602120 | tf_op jit(solution)/shard_map/ppermute | solution.py:43
  338.6 14.0 %collective-permute-start.49 = (bf16[2,2,2,64,512]{4,3,0,1,2:T(8,128)(2,1)S(1)}, bf16[2,2,2,64,512]{4,3,0,1,2:T(8,128)(2,1)S(1)}, u32[]{:S(2)}, u32[]{:S(2)}) collective-permute-start(bf16[2,2,2,64,512]{4,3,0,1,2:T(8,128)(2,1)S(1)} %dynamic-slice_bitcast_fusion), channel_id=1, source_target_pairs={{0,4},{4,0},{8,12},{12,8},{16,20},{20,16},{24,28},{28,24},{1,5},{5... | collective-permute-start | bytes 1572872 | tf_op jit(solution)/shard_map/ppermute | solution.py:33
  341.8 11.1 %collective-permute-start.44 = (bf16[2,2,2,16,2048]{4,3,0,1,2:T(8,128)(2,1)S(1)}, bf16[2,2,2,16,2048]{4,3,0,1,2:T(8,128)(2,1)S(1)}, u32[]{:S(2)}, u32[]{:S(2)}) collective-permute-start(bf16[2,2,2,16,2048]{4,3,0,1,2:T(8,128)(2,1)S(1)} %dynamic-slice_bitcast_fusion.1), channel_id=1, source_target_pairs={{0,2},{1,3},{2,0},{3,1},{4,6},{5,7},{6,4},{7,5},{8,10},{9,11},{10,... | collective-permute-start | bytes 1572872 | tf_op jit(solution)/shard_map/ppermute | solution.py:33
  348.5 14.9 %collective-permute-start.34 = (bf16[2,2,2,64,512]{4,3,0,1,2:T(8,128)(2,1)S(1)}, bf16[2,2,2,64,512]{4,3,0,1,2:T(8,128)(2,1)S(1)}, u32[]{:S(2)}, u32[]{:S(2)}) collective-permute-start(bf16[2,2,2,64,512]{4,3,0,1,2:T(8,128)(2,1)S(1)} %dynamic-slice_bitcast_fusion.2), channel_id=1, source_target_pairs={{0,4},{4,0},{8,12},{12,8},{16,20},{20,16},{24,28},{28,24},{1,5},{5... | collective-permute-start | bytes 1572872 | tf_op jit(solution)/shard_map/ppermute | solution.py:33
  349.9 16.2 %collective-permute-start.29 = (bf16[2,2,2,16,2048]{4,3,0,1,2:T(8,128)(2,1)S(1)}, bf16[2,2,2,16,2048]{4,3,0,1,2:T(8,128)(2,1)S(1)}, u32[]{:S(2)}, u32[]{:S(2)}) collective-permute-start(bf16[2,2,2,16,2048]{4,3,0,1,2:T(8,128)(2,1)S(1)} %dynamic-slice_bitcast_fusion.3), channel_id=1, source_target_pairs={{0,2},{1,3},{2,0},{3,1},{4,6},{5,7},{6,4},{7,5},{8,10},{9,11},{10,... | collective-permute-start | bytes 1572872 | tf_op jit(solution)/shard_map/ppermute | solution.py:33
  352.7 18.2 %collective-permute-start.50 = (bf16[2,2,64,512]{3,2,0,1:T(8,128)(2,1)S(1)}, bf16[2,2,64,512]{3,2,0,1:T(8,128)(2,1)S(1)}, u32[]{:S(2)}, u32[]{:S(2)}) collective-permute-start(bf16[2,2,64,512]{3,2,0,1:T(8,128)(2,1)S(1)} %dynamic-slice_bitcast_fusion.4), channel_id=1, source_target_pairs={{0,2},{1,3},{2,0},{3,1},{4,6},{5,7},{6,4},{7,5},{8,10},{9,11},{10,... | collective-permute-start | bytes 786440 | tf_op jit(solution)/shard_map/ppermute | solution.py:33
  353.0 16.0 %collective-permute-start.45 = (bf16[2,2,16,2048]{3,2,0,1:T(8,128)(2,1)S(1)}, bf16[2,2,16,2048]{3,2,0,1:T(8,128)(2,1)S(1)}, u32[]{:S(2)}, u32[]{:S(2)}) collective-permute-start(bf16[2,2,16,2048]{3,2,0,1:T(8,128)(2,1)S(1)} %dynamic-slice_bitcast_fusion.5), channel_id=1, source_target_pairs={{0,4},{4,0},{8,12},{12,8},{16,20},{20,16},{24,28},{28,24},{1,5},{5... | collective-permute-start | bytes 786440 | tf_op jit(solution)/shard_map/ppermute | solution.py:33
  363.5 19.9 %collective-permute-start.35 = (bf16[2,2,64,512]{3,2,0,1:T(8,128)(2,1)S(1)}, bf16[2,2,64,512]{3,2,0,1:T(8,128)(2,1)S(1)}, u32[]{:S(2)}, u32[]{:S(2)}) collective-permute-start(bf16[2,2,64,512]{3,2,0,1:T(8,128)(2,1)S(1)} %dynamic-slice_bitcast_fusion.6), channel_id=1, source_target_pairs={{0,2},{1,3},{2,0},{3,1},{4,6},{5,7},{6,4},{7,5},{8,10},{9,11},{10,... | collective-permute-start | bytes 786440 | tf_op jit(solution)/shard_map/ppermute | solution.py:33
  366.3 19.6 %collective-permute-start.30 = (bf16[2,2,16,2048]{3,2,0,1:T(8,128)(2,1)S(1)}, bf16[2,2,16,2048]{3,2,0,1:T(8,128)(2,1)S(1)}, u32[]{:S(2)}, u32[]{:S(2)}) collective-permute-start(bf16[2,2,16,2048]{3,2,0,1:T(8,128)(2,1)S(1)} %dynamic-slice_bitcast_fusion.7), channel_id=1, source_target_pairs={{0,4},{4,0},{8,12},{12,8},{16,20},{20,16},{24,28},{28,24},{1,5},{5... | collective-permute-start | bytes 786440 | tf_op jit(solution)/shard_map/ppermute | solution.py:33
  369.1 5.6 %collective-permute-start.46 = (bf16[2,16,2048]{2,1,0:T(8,128)(2,1)S(1)}, bf16[2,16,2048]{2,1,0:T(8,128)(2,1)S(1)}, u32[]{:S(2)}, u32[]{:S(2)}) collective-permute-start(bf16[2,16,2048]{2,1,0:T(8,128)(2,1)S(1)} %dynamic-slice_bitcast_fusion.9), channel_id=1, source_target_pairs={{0,8},{4,12},{8,0},{12,4},{16,24},{20,28},{24,16},{28,20},{1,9},{5... | collective-permute-start | bytes 393224 | tf_op jit(solution)/shard_map/ppermute | solution.py:33
  371.0 6.3 %collective-permute-start.51 = (bf16[2,64,512]{2,1,0:T(8,128)(2,1)S(1)}, bf16[2,64,512]{2,1,0:T(8,128)(2,1)S(1)}, u32[]{:S(2)}, u32[]{:S(2)}) collective-permute-start(bf16[2,64,512]{2,1,0:T(8,128)(2,1)S(1)} %dynamic-slice_bitcast_fusion.8), channel_id=1, source_target_pairs={{0,8},{4,12},{8,0},{12,4},{16,24},{20,28},{24,16},{28,20},{1,9},{5... | collective-permute-start | bytes 393224 | tf_op jit(solution)/shard_map/ppermute | solution.py:33
  374.7 5.5 %collective-permute-start.47 = (bf16[16,2048]{1,0:T(8,128)(2,1)S(1)}, bf16[16,2048]{1,0:T(8,128)(2,1)S(1)}, u32[]{:S(2)}, u32[]{:S(2)}) collective-permute-start(bf16[16,2048]{1,0:T(8,128)(2,1)S(1)} %dynamic-slice_bitcast_fusion.13), channel_id=1, source_target_pairs={{0,16},{4,20},{8,24},{12,28},{16,0},{20,4},{24,8},{28,12},{1,17},{... | collective-permute-start | bytes 196616 | tf_op jit(solution)/shard_map/ppermute | solution.py:33
  377.4 5.3 %collective-permute-start.52 = (bf16[64,512]{1,0:T(8,128)(2,1)S(1)}, bf16[64,512]{1,0:T(8,128)(2,1)S(1)}, u32[]{:S(2)}, u32[]{:S(2)}) collective-permute-start(bf16[64,512]{1,0:T(8,128)(2,1)S(1)} %dynamic-slice_bitcast_fusion.12), channel_id=1, source_target_pairs={{0,16},{4,20},{8,24},{12,28},{16,0},{20,4},{24,8},{28,12},{1,17},{... | collective-permute-start | bytes 196616 | tf_op jit(solution)/shard_map/ppermute | solution.py:33
  383.6 5.7 %collective-permute-start.36 = (bf16[2,64,512]{2,1,0:T(8,128)(2,1)S(1)}, bf16[2,64,512]{2,1,0:T(8,128)(2,1)S(1)}, u32[]{:S(2)}, u32[]{:S(2)}) collective-permute-start(bf16[2,64,512]{2,1,0:T(8,128)(2,1)S(1)} %dynamic-slice_bitcast_fusion.10), channel_id=1, source_target_pairs={{0,8},{4,12},{8,0},{12,4},{16,24},{20,28},{24,16},{28,20},{1,9},{5... | collective-permute-start | bytes 393224 | tf_op jit(solution)/shard_map/ppermute | solution.py:33
  386.0 5.9 %collective-permute-start.31 = (bf16[2,16,2048]{2,1,0:T(8,128)(2,1)S(1)}, bf16[2,16,2048]{2,1,0:T(8,128)(2,1)S(1)}, u32[]{:S(2)}, u32[]{:S(2)}) collective-permute-start(bf16[2,16,2048]{2,1,0:T(8,128)(2,1)S(1)} %dynamic-slice_bitcast_fusion.11), channel_id=1, source_target_pairs={{0,8},{4,12},{8,0},{12,4},{16,24},{20,28},{24,16},{28,20},{1,9},{5... | collective-permute-start | bytes 393224 | tf_op jit(solution)/shard_map/ppermute | solution.py:33
  389.3 5.2 %collective-permute-start.37 = (bf16[64,512]{1,0:T(8,128)(2,1)S(1)}, bf16[64,512]{1,0:T(8,128)(2,1)S(1)}, u32[]{:S(2)}, u32[]{:S(2)}) collective-permute-start(bf16[64,512]{1,0:T(8,128)(2,1)S(1)} %dynamic-slice_bitcast_fusion.14), channel_id=1, source_target_pairs={{0,16},{4,20},{8,24},{12,28},{16,0},{20,4},{24,8},{28,12},{1,17},{... | collective-permute-start | bytes 196616 | tf_op jit(solution)/shard_map/ppermute | solution.py:33
  392.0 5.9 %collective-permute-start.32 = (bf16[16,2048]{1,0:T(8,128)(2,1)S(1)}, bf16[16,2048]{1,0:T(8,128)(2,1)S(1)}, u32[]{:S(2)}, u32[]{:S(2)}) collective-permute-start(bf16[16,2048]{1,0:T(8,128)(2,1)S(1)} %dynamic-slice_bitcast_fusion.15), channel_id=1, source_target_pairs={{0,16},{4,20},{8,24},{12,28},{16,0},{20,4},{24,8},{28,12},{1,17},{... | collective-permute-start | bytes 196616 | tf_op jit(solution)/shard_map/ppermute | solution.py:33
  (294 other events, 1304.0 us)
